TPU v7x, 512 devices: a whole 4x8x8 slice. The times are simulated.
512 devices in a mesh: section: 16 (over z, y_lo), seq: 32 (over x, y_hi, core).
Axes of the slice: x: 4, y: 8 (y_hi: 4, y_lo: 2; y = y_hi * 2 + y_lo), z: 8, core: 2. Of those that a mesh axis runs over, the one named last changes fastest.
Arguments:
- forward_input: bfloat16 [16, 4096, 1024], P('section', 'seq'), may hold values from -6 to 6
- stored_input: bfloat16 [16, 4096, 1024], P('section', 'seq'), may hold values from -6 to 6
- output_cotangent: bfloat16 [16, 4096, 1024], P('section', 'seq'), may hold values from -6 to 6
- norm_gain: float32 [16, 1024], P('section'), may hold values from 0.5 to 2
- query_weight: bfloat16 [16, 1024, 512], P('section'), may hold values from -0.325 to 0.325
- key_weight: bfloat16 [16, 1024, 128], P('section'), may hold values from -7.3125 to 7.3125
- value_weight: bfloat16 [16, 1024, 128], P('section'), may hold values from -0.1875 to 0.1875
- output_weight: bfloat16 [16, 512, 1024], P('section'), may hold values from -0.25 to 0.25
- frame_index: int32 [4096], replicated, may hold values from 0 to 15, as said below
- valid_counts: int32 [32], replicated, may hold values from 32 to 128
Outputs:
- forward_next: bfloat16 [16, 4096, 1024], P('section', 'seq')
- backward_next: bfloat16 [16, 4096, 1024], P('section', 'seq')
Inputs may be any that keep to these rules, and one draw needn't show every extreme that they name: `frame_index`: frame numbers start at 0, never fall along the sequence, and every number up to the largest occurs.
All inputs are finite; a program needn't handle non-finite values.
Results may differ from a plain program's by a relative error of at most 0.028.
The roundings to bfloat16 on the way count: a program that leaves them out, or rounds other values in their place, can miss the bound.
Values may be sent and summed in bfloat16 or wider, within the bound.
A program may use at most 64 MiB of HBM per device.

v0:
```python
from functools import partial
import math

import jax
import jax.numpy as jnp
from jax import lax
from jax.sharding import PartitionSpec as P

HEADS = 8
KV_HEADS = 2
HEAD_DIM = 64


NORM_EPSILON = 1e-05
MASKED_SCORE = -1e30


def side_by_side(arrays, axis, dim, along):
    both = jnp.concatenate(arrays, axis=along)
    whole, at, gathered = (lax.all_gather(both, axis, axis=dim, tiled=True), 0, [])
    for a in arrays:
        gathered.append(lax.slice_in_dim(whole, at, at + a.shape[along], axis=along))
        at += a.shape[along]
    return tuple(gathered)


def shifted(block, axis, distance):
    devices = range(lax.axis_size(axis))
    route = [((i - distance) % len(devices), i) for i in devices]
    return lax.ppermute(block, axis, route)


def normalize(inputs, norm_scale):
    widened = inputs.astype(jnp.float32)
    inverse = lax.rsqrt(jnp.mean(widened * widened, axis=-1, keepdims=True) + NORM_EPSILON)
    return ((widened * inverse * norm_scale).astype(jnp.bfloat16), inverse)


def project(normed, weight):
    return jnp.dot(normed, weight, preferred_element_type=jnp.float32).astype(jnp.bfloat16)


def project_back(gradient, weight):
    return lax.dot_general(
        gradient, weight, (((1,), (1,)), ((), ())), preferred_element_type=jnp.float32
    )


def valid_table(valid_counts, slice_rows):
    inside = jnp.arange(slice_rows, dtype=jnp.int32)
    return (inside[None, :] < valid_counts[:, None]).reshape(-1)


def key_visible(query_frames, frame_index, valid_flags, first_row, key_rows):
    key_frames = lax.dynamic_slice_in_dim(frame_index, first_row, key_rows)
    key_valid = lax.dynamic_slice_in_dim(valid_flags, first_row, key_rows)
    return key_valid[None, :] & (key_frames[None, :] <= query_frames[:, None])


def fold_blocks(update, carried, members, first_row):
    row_count = members[0].shape[0]
    block_rows = math.gcd(row_count, 512)
    blocks = row_count // block_rows
    stacked = tuple((member.reshape((blocks, block_rows) + member.shape[1:]) for member in members))

    def fold_advance(state, item):
        block_index, pieces = item
        return (update(state, pieces, first_row + block_index * block_rows, block_rows), None)

    carried, _ = lax.scan(fold_advance, carried, (jnp.arange(blocks, dtype=jnp.int32), stacked))
    return carried


def attend(
    queries,
    query_frames,
    frame_index,
    valid_flags,
    score_scale,
    state,
    pieces,
    first_row,
    block_rows,
):

    def attend_compute(state):
        running_max, running_sum, weighted = state
        key_block, value_block = pieces
        groups = queries.shape[1]
        key_heads = key_block.reshape(block_rows, groups, -1)
        value_heads = value_block.reshape(block_rows, groups, -1)
        scores = (
            jnp.einsum("cgrd,kgd->grck", queries, key_heads, preferred_element_type=jnp.float32)
            * score_scale
        )
        visible = key_visible(query_frames, frame_index, valid_flags, first_row, block_rows)
        scores = jnp.where(visible, scores, MASKED_SCORE)
        new_max = jnp.maximum(running_max, jnp.max(scores, axis=-1))
        weights = jnp.where(visible, jnp.exp(scores - new_max[..., None]), 0.0)
        factor = jnp.exp(running_max - new_max)
        running_sum = running_sum * factor + jnp.sum(weights, axis=-1)
        weighted = weighted * factor[..., None] + jnp.einsum(
            "grck,kgd->grcd",
            weights.astype(jnp.bfloat16),
            value_heads,
            preferred_element_type=jnp.float32,
        )
        return (new_max, running_sum, weighted)

    beyond = frame_index[first_row] > query_frames[-1]
    return lax.cond(beyond, lambda state: state, attend_compute, state)


def finish(state, slice_rows):
    running_max, running_sum, weighted = state
    attended = weighted / running_sum[..., None]
    return (
        attended.transpose(2, 0, 1, 3).reshape(slice_rows, -1).astype(jnp.bfloat16),
        running_max + jnp.log(running_sum),
    )


def local_backward(
    query_heads,
    dout_heads,
    log_sums,
    deltas,
    query_frames,
    frame_index,
    valid_flags,
    score_scale,
    all_keys,
    all_values,
):
    row_count = all_keys.shape[0]
    block_rows = math.gcd(row_count, 512)
    blocks = row_count // block_rows
    groups = query_heads.shape[1]
    key_stack = all_keys.reshape(blocks, block_rows, groups, -1)
    value_stack = all_values.reshape(blocks, block_rows, groups, -1)
    head_size = key_stack.shape[-1]

    def local_advance(query_grad, item):
        block_index, key_heads, value_heads = item
        first_row = block_index * block_rows

        def local_compute(query_grad):
            scores = (
                jnp.einsum(
                    "cgrd,kgd->grck", query_heads, key_heads, preferred_element_type=jnp.float32
                )
                * score_scale
            )
            visible = key_visible(query_frames, frame_index, valid_flags, first_row, block_rows)
            scores = jnp.where(visible, scores, MASKED_SCORE)
            probability = jnp.where(visible, jnp.exp(scores - log_sums[..., None]), 0.0)
            prob_grads = jnp.einsum(
                "cgrd,kgd->grck", dout_heads, value_heads, preferred_element_type=jnp.float32
            )
            score_grads = (probability * (prob_grads - deltas[..., None])).astype(jnp.bfloat16)
            query_grad = query_grad + jnp.einsum(
                "grck,kgd->cgrd", score_grads, key_heads, preferred_element_type=jnp.float32
            )
            key_grad = (
                jnp.einsum(
                    "grck,cgrd->kgd", score_grads, query_heads, preferred_element_type=jnp.float32
                )
                * score_scale
            )
            value_grad = jnp.einsum(
                "grck,cgrd->kgd",
                probability.astype(jnp.bfloat16),
                dout_heads,
                preferred_element_type=jnp.float32,
            )
            return (
                query_grad,
                (key_grad.reshape(block_rows, -1), value_grad.reshape(block_rows, -1)),
            )

        def skipped(query_grad):
            empty = jnp.zeros((block_rows, groups * head_size), jnp.float32)
            return (query_grad, (empty, empty))

        beyond = frame_index[first_row] > query_frames[-1]
        return lax.cond(beyond, skipped, local_compute, query_grad)

    start_grad = jnp.zeros(query_heads.shape, jnp.float32)
    query_grad, terms = lax.scan(
        local_advance, start_grad, (jnp.arange(blocks, dtype=jnp.int32), key_stack, value_stack)
    )
    return (query_grad, (terms[0].reshape(row_count, -1), terms[1].reshape(row_count, -1)))


def on_device(
    forward_input,
    stored_input,
    output_cotangent,
    norm_gain,
    query_weight,
    key_weight,
    value_weight,
    output_weight,
    frame_index,
    valid_counts,
):
    slice_rows = forward_input.shape[1]
    group_size = HEADS // KV_HEADS
    score_scale = 1.0 / math.sqrt(HEAD_DIM)
    norm_scale = norm_gain[0]
    query_proj = query_weight[0]
    key_proj = key_weight[0]
    value_proj = value_weight[0]
    out_proj = output_weight[0]
    own_first = lax.axis_index("seq") * slice_rows
    query_frames = lax.dynamic_slice_in_dim(frame_index, own_first, slice_rows)
    valid_flags = valid_table(valid_counts, slice_rows)
    fwd_inputs = forward_input[0]
    normed_fwd, _ = normalize(fwd_inputs, norm_scale)
    query_fwd = project(normed_fwd, query_proj).reshape(slice_rows, KV_HEADS, group_size, HEAD_DIM)
    keys_fwd = project(normed_fwd, key_proj)
    values_fwd = project(normed_fwd, value_proj)
    bwd_inputs = stored_input[0]
    normed_bwd, inverse_bwd = normalize(bwd_inputs, norm_scale)
    query_flat = project(normed_bwd, query_proj)
    query_bwd = query_flat.reshape(slice_rows, KV_HEADS, group_size, HEAD_DIM)
    keys_bwd = project(normed_bwd, key_proj)
    values_bwd = project(normed_bwd, value_proj)
    state_shape = (KV_HEADS, group_size, slice_rows)
    empty_state = (
        jnp.full(state_shape, MASKED_SCORE, jnp.float32),
        jnp.zeros(state_shape, jnp.float32),
        jnp.zeros(state_shape + (HEAD_DIM,), jnp.float32),
    )
    attend_fwd = partial(attend, query_fwd, query_frames, frame_index, valid_flags, score_scale)
    attend_bwd = partial(attend, query_bwd, query_frames, frame_index, valid_flags, score_scale)
    state_fwd = (
        lambda carried, pieces, first_row: fold_blocks(attend_fwd, carried, pieces, first_row)
    )(empty_state, side_by_side((keys_fwd, values_fwd), "seq", 0, 1), jnp.int32(0))
    all_keys_bwd, all_values_bwd = side_by_side((keys_bwd, values_bwd), "seq", 0, 1)
    attended_fwd, _ = finish(state_fwd, slice_rows)
    layer_out = (
        fwd_inputs.astype(jnp.float32)
        + jnp.dot(attended_fwd, out_proj, preferred_element_type=jnp.float32)
    ).astype(jnp.bfloat16)
    forward_next = shifted(layer_out, "section", 1)
    state_bwd = fold_blocks(attend_bwd, empty_state, (all_keys_bwd, all_values_bwd), 0)
    attended_bwd, log_sums = finish(state_bwd, slice_rows)
    cotangent = output_cotangent[0]
    dout = project_back(cotangent, out_proj).astype(jnp.bfloat16)
    dout_heads = dout.reshape(slice_rows, KV_HEADS, group_size, HEAD_DIM)
    attended_heads = attended_bwd.reshape(slice_rows, KV_HEADS, group_size, HEAD_DIM)
    deltas = jnp.sum(
        dout_heads.astype(jnp.float32) * attended_heads.astype(jnp.float32), axis=-1
    ).transpose(1, 2, 0)
    query_grad, key_value_terms = local_backward(
        query_bwd,
        dout_heads,
        log_sums,
        deltas,
        query_frames,
        frame_index,
        valid_flags,
        score_scale,
        all_keys_bwd,
        all_values_bwd,
    )
    key_grad, value_grad = lax.psum_scatter(key_value_terms, "seq", scatter_dimension=0, tiled=True)
    query_grad = (query_grad * score_scale).astype(jnp.bfloat16).reshape(slice_rows, -1)
    normed_grad = project_back(query_grad, query_proj)
    normed_grad = normed_grad + project_back(key_grad.astype(jnp.bfloat16), key_proj)
    normed_grad = normed_grad + project_back(value_grad.astype(jnp.bfloat16), value_proj)
    scaled_grad = normed_grad * norm_scale
    widened = bwd_inputs.astype(jnp.float32)
    input_grad = (
        cotangent.astype(jnp.float32)
        + inverse_bwd * scaled_grad
        - widened * inverse_bwd**3 * jnp.mean(widened * scaled_grad, axis=-1, keepdims=True)
    )
    backward_next = shifted(input_grad.astype(jnp.bfloat16), "section", -1)
    return (forward_next[None], backward_next[None])


def solution(mesh):
    return jax.shard_map(
        on_device,
        mesh=mesh,
        in_specs=(
            P("section", "seq", None),
            P("section", "seq", None),
            P("section", "seq", None),
            P("section", None),
            P("section", None, None),
            P("section", None, None),
            P("section", None, None),
            P("section", None, None),
            P(),
            P(),
        ),
        out_specs=(P("section", "seq", None), P("section", "seq", None)),
        check_vma=False,
    )
```

profile of v0, /device:TPU:1, one launch (start us, length us, event | category | flops | bytes accessed | tf_op | source)
XLA Modules:
  0.0 443.0 jit_solution(10390311697203848460)
XLA Ops:
  8.5 1.4 convolution_convert_fusion.3
  9.9 1.5 convolution_convert_fusion.4
  13.1 1.4 convolution_convert_fusion.5
  16.9 62.8 %all-gather.5.cloned.1.call-done = bf16[4096,256]{0,1:T(8,128)(2,1)} async-done(((bf16[128,256]{0,1:T(8,128)(2,1)}), bf16[4096,256]{0,1:T(8,128)(2,1)}) %all-gather.5.cloned.1.call-update) | async-done | bytes 2097168 | tf_op jit(solution)/shard_map/all_gather | solution.py:20
  79.7 1.7 fusion.91
  81.4 1.7 copy_bitcast_fusion
  83.1 32.9 %while.49 = (s32[]{:T(128)}, f32[2,4,128]{2,1,0:T(4,128)S(1)}, f32[2,4,128]{2,1,0:T(4,128)S(1)}, f32[2,4,128,64]{2,3,1,0:T(8,128)S(1)}, s32[8]{0:T(128)S(1)}, /*...) while((s32[]{:T(128)}, f32[2,4,128]{2,1,0:T(4,128)S(1)}, ...), condition=%wide.region_13.14_spmd.clone, body=%wide.region_8.13_spmd.clone.sunk | while | flops 141301760 | bytes 8073759 | solution.py:70
  86.8 3.1 conditional.10
  116.0 1.6 copy.69
  117.6 1.3 copy.40
  119.3 1.4 copy.41
  120.8 46.2 %while.50 = (s32[]{:T(128)}, f32[128,2,4,64]{0,3,2,1:T(8,128)S(1)}, f32[8,512,128]{2,1,0:T(8,128)}, f32[8,512,128]{2,1,0:T(8,128)}, s32[8]{0:T(128)S(1)}, /*inde...) while((s32[]{:T(128)}, f32[128,2,4,64]{0,3,2,1:T(8,128)S(1)}, ...), condition=%wide.region_18.19_spmd.clone, body=%wide.region_15.18_spmd.clone.sunk | while | flops 340004864 | bytes 13654563 | solution.py:189
  124.7 5.5 %conditional.11 = (f32[128,2,4,64]{0,3,2,1:T(8,128)S(1)}, f32[1,512,128]{1,2,0:T(8,128)S(1)}, f32[1,512,128]{1,2,0:T(8,128)S(1)}) conditional(s32[]{:T(128)} %bitcast.254, (s32[]{:T(128)}, pred[4096]{0:T(1024)(128)(4,1)S(1)}, s32[4096]{0:T(1024)S(1)}, s32[128]{0:T(128)S(1)}, bf16[8,512,2,64]{1,3,2,0:T(8,128)(2,1)}, /*index=5*/s32[]{:T(128)}, ...), branch_computations={%region_16.16_spmd, %region_17.17_spmd} | conditional | flops 340000768 | bytes 11552322 | solution.py:186
  125.1 1.6 fusion.32
  126.7 1.4 fusion.29
  167.6 1.7 fusion.92
  169.3 1.6 copy_bitcast_fusion.2
  170.9 34.4 %while.48 = (s32[]{:T(128)}, f32[2,4,128]{2,1,0:T(4,128)S(1)}, f32[2,4,128]{2,1,0:T(4,128)S(1)}, f32[2,4,128,64]{2,3,1,0:T(8,128)S(1)}, s32[8]{0:T(128)S(1)}, /*...) while((s32[]{:T(128)}, f32[2,4,128]{2,1,0:T(4,128)S(1)}, ...), condition=%wide.region_6.7_spmd.clone, body=%wide.region_1.6_spmd.clone.sunk | while | flops 141301760 | bytes 8073759 | solution.py:70
  174.8 3.1 conditional.9
  205.7 1.9 collective-permute-start
  207.7 114.4 %reduce-scatter.5.cloned.1.call-done = f32[128,128]{1,0:T(8,128)} async-done(((f32[4096,128]{1,0:T(8,128)}), f32[128,128]{1,0:T(8,128)}) %reduce-scatter.5.cloned.1.call-update) | async-done | bytes 65552 | tf_op jit(solution)/shard_map/reduce_scatter | solution.py:268
  323.3 100.7 %reduce-scatter.3.cloned.1.call-done = f32[128,128]{1,0:T(8,128)} async-done(((f32[4096,128]{1,0:T(8,128)}), f32[128,128]{1,0:T(8,128)}) %reduce-scatter.3.cloned.1.call-update) | async-done | bytes 65552 | tf_op jit(solution)/shard_map/reduce_scatter | solution.py:268
  426.1 5.6 %collective-permute-start.1 = (bf16[128,1024]{1,0:T(8,128)(2,1)S(1)}, bf16[128,1024]{1,0:T(8,128)(2,1)S(1)}, u32[]{:S(2)}, u32[]{:S(2)}) collective-permute-start(bf16[128,1024]{1,0:T(8,128)(2,1)S(1)} %fusion.67), channel_id=1, source_target_pairs={{32,0},{64,32},{96,64},{128,96},{160,128},{192,160},{224,192},{256... | collective-permute-start | bytes 786440 | tf_op jit(solution)/shard_map/ppermute | solution.py:30
  431.8 3.3 collective-permute-done.1
  (282 shorter events, 75.3 us)
Async XLA Ops:
  7.2 8.5 %copy-start = (bf16[1,1024,512]{2,1,0:T(8,128)(2,1)S(1)}, bf16[1,1024,512]{2,1,0:T(8,128)(2,1)}, u32[]{:S(2)}) copy-start(bf16[1,1024,512]{2,1,0:T(8,128)(2,1)} %param.26) | copy-start | bytes 3145732
  7.2 8.5 %copy-start.4 = (bf16[1,128,1024]{2,1,0:T(8,128)(2,1)S(1)}, bf16[1,128,1024]{2,1,0:T(8,128)(2,1)}, u32[]{:S(2)}) copy-start(bf16[1,128,1024]{2,1,0:T(8,128)(2,1)} %param.23) | copy-start | bytes 786436
  7.2 7.3 %copy-start.11 = (f32[1,1024]{1,0:T(1,128)S(1)}, f32[1,1024]{1,0:T(1,128)}, u32[]{:S(2)}) copy-start(f32[1,1024]{1,0:T(1,128)} %param.25) | copy-start | bytes 12292
  7.2 7.3 %copy-start.8 = (bf16[1,1024,128]{2,1,0:T(8,128)(2,1)S(1)}, bf16[1,1024,128]{2,1,0:T(8,128)(2,1)}, u32[]{:S(2)}) copy-start(bf16[1,1024,128]{2,1,0:T(8,128)(2,1)} %param.27) | copy-start | bytes 786436
  7.2 7.3 %copy-start.5 = (bf16[1,128,1024]{2,1,0:T(8,128)(2,1)S(1)}, bf16[1,128,1024]{2,1,0:T(8,128)(2,1)}, u32[]{:S(2)}) copy-start(bf16[1,128,1024]{2,1,0:T(8,128)(2,1)} %param.22) | copy-start | bytes 786436
  7.2 72.4 %all-gather.5.cloned.1.call-start = ((), (), s32[]{:S(2)}) async-start(), calls=%async_computation.3 | async-start | bytes 2162688 | tf_op jit(solution)/shard_map/all_gather | solution.py:20
  9.9 6.3 %copy-start.2 = (bf16[1,512,1024]{2,1,0:T(8,128)(2,1)S(1)}, bf16[1,512,1024]{2,1,0:T(8,128)(2,1)}, u32[]{:S(2)}) copy-start(bf16[1,512,1024]{2,1,0:T(8,128)(2,1)} %param.29) | copy-start | bytes 3145732
  9.9 6.3 %copy-start.6 = (bf16[1,128,1024]{2,1,0:T(8,128)(2,1)S(1)}, bf16[1,128,1024]{2,1,0:T(8,128)(2,1)}, u32[]{:S(2)}) copy-start(bf16[1,128,1024]{2,1,0:T(8,128)(2,1)} %param.24) | copy-start | bytes 786436
  12.0 155.6 %all-gather.3.cloned.1.call-start = ((), (), s32[]{:S(2)}) async-start(), calls=%async_computation.2 | async-start | bytes 2162688 | tf_op jit(solution)/shard_map/all_gather | solution.py:20
  14.5 2.2 copy-start.10
  15.5 306.5 %reduce-scatter.5.cloned.1.call-start = ((), (), s32[]{:S(2)}) async-start(), calls=%async_computation.5 | async-start | bytes 2162688 | tf_op jit(solution)/shard_map/reduce_scatter | solution.py:268
  81.3 1.7 copy-start.1
  81.3 1.8 copy-start.9
  167.0 257.1 %reduce-scatter.3.cloned.1.call-start = ((), (), s32[]{:S(2)}) async-start(), calls=%async_computation.4 | async-start | bytes 2162688 | tf_op jit(solution)/shard_map/reduce_scatter | solution.py:268
  170.9 34.5 %copy-start.3 = (bf16[1,512,1024]{2,1,0:T(8,128)(2,1)S(1)}, bf16[1,512,1024]{2,1,0:T(8,128)(2,1)}, u32[]{:S(2)}) copy-start(bf16[1,512,1024]{2,1,0:T(8,128)(2,1)} %param.29) | copy-start | bytes 3145732
  205.7 226.1 %collective-permute-start = (bf16[128,1024]{1,0:T(8,128)(2,1)S(1)}, bf16[128,1024]{1,0:T(8,128)(2,1)S(1)}, u32[]{:S(2)}, u32[]{:S(2)}) collective-permute-start(bf16[128,1024]{1,0:T(8,128)(2,1)S(1)} %fusion.51), channel_id=1, source_target_pairs={{480,0},{0,32},{32,64},{64,96},{96,128},{128,160},{160,192},{192,2... | collective-permute-start | bytes 786440 | tf_op jit(solution)/shard_map/ppermute | solution.py:30
  323.3 102.6 %copy-start.7 = (bf16[1,128,1024]{2,1,0:T(8,128)(2,1)S(1)}, bf16[1,128,1024]{2,1,0:T(8,128)(2,1)}, u32[]{:S(2)}) copy-start(bf16[1,128,1024]{2,1,0:T(8,128)(2,1)} %param.24) | copy-start | bytes 786436
  426.1 8.9 %collective-permute-start.1 = (bf16[128,1024]{1,0:T(8,128)(2,1)S(1)}, bf16[128,1024]{1,0:T(8,128)(2,1)S(1)}, u32[]{:S(2)}, u32[]{:S(2)}) collective-permute-start(bf16[128,1024]{1,0:T(8,128)(2,1)S(1)} %fusion.67), channel_id=1, source_target_pairs={{32,0},{64,32},{96,64},{128,96},{160,128},{192,160},{224,192},{256... | collective-permute-start | bytes 786440 | tf_op jit(solution)/shard_map/ppermute | solution.py:30
Sparse Core Ops, SparseCore 0:
  12.1 67.4 all-gather.4
  83.3 59.2 all-gather.2
  167.1 154.9 reduce-scatter.4
  326.3 97.6 reduce-scatter.2
where the time goes:
time: 446 us; the launch traced here: 443 us
  waiting for transfers between devices  281 us (63%)
  local copies, waits for them, and re-layouts  68.9 us (15%)
  loops' own time  47 us (11%)
  matrix products  16.4 us (4%)
  between operations  14.2 us (3%)
  starting transfers between devices  7.71 us (2%)
  other arithmetic  7.43 us (2%)
    reduce_scatter x2, waiting for transfers between devices, on_device(): lax.psum_scatter(key_value_terms, 'seq', scatter_dimension=0, tiled=True)  215 us
    all_gather x2, waiting for transfers between devices, side_by_side(): lax.all_gather(both, axis, axis=dim, tiled=True)  62.8 us
    another operation x2, loops' own time, fold_blocks(): lax.scan(fold_advance, carried, (jnp.arange(blocks, dtype=jnp.int32), sta...  30.9 us
    dynamic_slice x26, local copies, waits for them, and re-layouts, fold_blocks(): lax.scan(fold_advance, carried, (jnp.arange(blocks, dtype=jnp.int32), sta...  16 us
    another operation x1, loops' own time, local_backward(): lax.scan(local_advance, start_grad, (jnp.arange(blocks, dtype=jnp.int32),...  15.9 us
    dynamic_slice x16, local copies, waits for them, and re-layouts, attend(): beyond = frame_index[first_row] > query_frames[-1]  9.96 us
    slice x16, local copies, waits for them, and re-layouts, attend(): beyond = frame_index[first_row] > query_frames[-1]  9.62 us
    unnamed x32, local copies, waits for them, and re-layouts  9.41 us
  transfers between devices with their start and end apart: 6, of which 4 were waited for; matrix products, arithmetic and copies ran while one was open for 20% of the time, Pallas kernels for 0%

commit v1 on v0

v1 whole, which is shorter than its diff:
```python
import functools
import math

import jax
import jax.numpy as jnp
from jax import lax
from jax.experimental import pallas as pl
from jax.experimental.pallas import tpu as pltpu
from jax.sharding import PartitionSpec as P

F32 = jnp.float32
BF16 = jnp.bfloat16
D = 1024
HEAD_DIM = 64
ROWS = 128
CHIP = 256
QROWS = 1024
KB = 512
NORM_EPSILON = 1e-05
MASKED = -1e30
FIRST_MAX = -1e20
NN = (((1,), (0,)), ((), ()))
NT = (((1,), (1,)), ((), ()))

OFFSET_X = (0, 1, 3, 2)
FORWARD_ORDER = ((0, 0), (0, 1), (1, 0), (2, 0), (1, 1), (2, 1), (3, 0), (3, 1))
BACKWARD_ORDER = ((3, 0), (3, 1), (1, 1), (2, 0), (1, 0), (2, 1), (0, 0), (0, 1))
MESSAGES = 40


def dot(a, b, dims):
    return lax.dot_general(a, b, dims, preferred_element_type=F32)


def fused(
    x_f, x_b, cot_in, gain, wq_in, wk_in, wv_in, wo_in, frames, counts,
    out_f, out_b,
    xf, xb, cot, wq, wkv, wo, nb,
    kvst_b, kvst_f, kvb, kvf, aux,
    qst_b, qst_f, dost, qxb, qxf, dox,
    ws_b, ws_f, wd, wkq, wvo,
    pa, pb, sa, sb, ta, tb, ua, ub,
    acc, accq, mrow, frow,
    dkv, d0, rxh, rxf, ryh, ryf, dfst, dfin,
    ost, att, dqst, dqx, stage_f, stage_b,
    load_sem, send_sem, recv_sem,
):
    sec = lax.axis_index("section")
    seq = lax.axis_index("seq")
    n_sec = lax.axis_size("section")
    x, yh, core = seq // 8, (seq // 2) % 4, seq % 2
    other = 1 - core

    def at(xx, yy, cc):
        return {"seq": (xx * 4 + yy) * 2 + cc}

    partner = at(x, yh, other)
    xp, xm = at((x + 1) % 4, yh, core), at((x + 3) % 4, yh, core)
    yp, ym = at(x, (yh + 1) % 4, core), at(x, (yh + 3) % 4, core)
    sp, sm = {"section": (sec + 1) % n_sec}, {"section": (sec + n_sec - 1) % n_sec}

    loads = []
    for i, (src, dst) in enumerate((
        (x_b, xb), (wk_in, wkv.at[:, 0:128]), (wv_in, wkv.at[:, 128:256]),
        (wq_in, wq), (cot_in, cot), (wo_in, wo), (x_f, xf),
    )):
        copy = pltpu.make_async_copy(src, dst, load_sem.at[i])
        copy.start()
        loads.append(copy)

    barrier = pltpu.get_barrier_semaphore()
    for dev in (partner, xp, xm, yp, ym, sp, sm):
        pl.semaphore_signal(barrier, inc=1, device_id=dev, device_id_type=pl.DeviceIdType.MESH)

    used = []

    def message(src, dst, dev):
        i = len(used)
        copy = pltpu.make_async_remote_copy(
            src_ref=src, dst_ref=dst, send_sem=send_sem.at[i], recv_sem=recv_sem.at[i],
            device_id=dev, device_id_type=pl.DeviceIdType.MESH,
        )
        used.append(copy)
        return copy

    mine = pl.ds(pl.multiple_of(core * ROWS, ROWS), ROWS)

    m_kvb = message(kvst_b.at[other], kvb.at[0, 0, mine], partner)
    m_kvf = message(kvst_f.at[other], kvf.at[0, 0, mine], partner)
    m_qb = message(qst_b.at[other], qxb.at[mine], partner)
    m_qf = message(qst_f.at[other], qxf.at[mine], partner)
    m_do = message(dost.at[other], dox.at[mine], partner)
    m_att = message(ost.at[other], att.at[core], partner)
    m_dq = message(dqst.at[other], dqx.at[core], partner)
    m_dkv = message(dfst.at[other], dfin.at[core], partner)

    class Gather:
        def __init__(self, kv):
            self.y = (message(kv.at[0, 0], kv.at[0, 3], yp), message(kv.at[0, 0], kv.at[0, 1], ym))
            self.y2 = (
                message(kv.at[0, 3, 0:128], kv.at[0, 2, 0:128], yp),
                message(kv.at[0, 1, 128:256], kv.at[0, 2, 128:256], ym),
            )
            self.x = tuple(
                (
                    message(kv.at[0, 2 * h:2 * h + 2], kv.at[2, 2 * h:2 * h + 2], xp),
                    message(kv.at[0, 2 * h:2 * h + 2], kv.at[1, 2 * h:2 * h + 2], xm),
                )
                for h in range(2)
            )
            self.x2 = (
                message(kv.at[2, 0:2], kv.at[3, 0:2], xp),
                message(kv.at[1, 2:4], kv.at[3, 2:4], xm),
            )

        def start(self):
            self.y[0].start()
            self.y[1].start()

        def step1(self):
            self.y[0].wait_recv()
            self.y[1].wait_recv()
            self.y2[0].start()
            self.y2[1].start()
            self.x[0][0].start()
            self.x[0][1].start()

        def step2(self):
            self.y2[0].wait_recv()
            self.y2[1].wait_recv()
            self.x[1][0].start()
            self.x[1][1].start()

        def step3(self):
            self.x[0][0].wait_recv()
            self.x2[0].start()
            self.x[0][1].wait_recv()

        def step4(self):
            self.x[1][1].wait_recv()
            self.x2[1].start()
            self.x[1][0].wait_recv()

    gather_b, gather_f = Gather(kvb), Gather(kvf)

    r_half = (message(dkv.at[3, 0:2], rxh.at[0], xp), message(dkv.at[3, 2:4], rxh.at[1], xm))
    r_full = {
        (1, h): message(dkv.at[1, 2 * h:2 * h + 2], rxf.at[0, h], xp) for h in range(2)
    } | {
        (2, h): message(dkv.at[2, 2 * h:2 * h + 2], rxf.at[1, h], xm) for h in range(2)
    }
    ry_half = (
        message(dkv.at[0, 2, 0:128], ryh.at[0], yp), message(dkv.at[0, 2, 128:256], ryh.at[1], ym),
    )
    ry_full = (message(dkv.at[0, 1], ryf.at[0], yp), message(dkv.at[0, 3], ryf.at[1], ym))

    m_out_f = message(stage_f, out_f, sp)
    m_out_b = message(stage_b, out_b, sm)
    assert len(used) == MESSAGES

    def normalize(inputs):
        wide = inputs[...].astype(F32)
        inverse = lax.rsqrt(jnp.mean(wide * wide, axis=-1, keepdims=True) + NORM_EPSILON)
        return (wide * inverse * gain[...]).astype(BF16), inverse

    def key_values(normed, staged, kv):
        both = dot(normed, wkv[...], NN)
        staged[0] = jnp.concatenate([both[:, 0:64], both[:, 128:192]], axis=1).astype(BF16)
        staged[1] = jnp.concatenate([both[:, 64:128], both[:, 192:256]], axis=1).astype(BF16)
        kv[0, 0, mine] = staged[core]

    def halves(value, staged, whole):
        staged[0] = value[:, 0:256].astype(BF16)
        staged[1] = value[:, 256:512].astype(BF16)
        whole[mine] = staged[core]

    loads[0].wait()
    normed_b, inverse_b = normalize(xb)
    nb[...] = normed_b
    loads[1].wait()
    loads[2].wait()
    key_values(nb[...], kvst_b, kvb)
    pl.semaphore_wait(barrier, 7)
    m_kvb.start()
    loads[3].wait()
    halves(dot(nb[...], wq[...], NN) * 0.125, qst_b, qxb)
    m_qb.start()
    m_kvb.wait_recv()
    gather_b.start()
    loads[4].wait()
    loads[5].wait()
    halves(dot(cot[...], wo[...], NT), dost, dox)
    m_do.start()
    gather_b.step1()

    loads[6].wait()
    normed_f, _ = normalize(xf)
    nb[...] = normed_f
    key_values(nb[...], kvst_f, kvf)
    m_kvf.start()

    chip = x * 4 + yh

    def mask_block(k, carry):
        pos, dy = k // 4, k % 4
        dx = jnp.where(pos == 2, 3, jnp.where(pos == 3, 2, pos))
        chip_k = ((x + dx) % 4) * 4 + (yh + dy) % 4
        number = lax.broadcasted_iota(jnp.int32, (128, 128), 0)
        lane = lax.broadcasted_iota(jnp.int32, (128, 128), 1)
        for h in range(2):
            row = frames[pl.ds(2 * chip_k + h, 1), :]
            seen = (row <= number) & (lane < counts[2 * chip_k + h])
            bias = jnp.where(seen | (number >= 16), 0.0, MASKED)
            aux[pos, dy, h * 128:(h + 1) * 128, :] = bias.T.astype(BF16)
        return carry

    lax.fori_loop(0, 16, mask_block, 0)

    number = lax.broadcasted_iota(jnp.int32, (128, 128), 0)
    one_hot = jnp.concatenate(
        [(frames[pl.ds(2 * chip + h, 1), :] == number).astype(F32) for h in range(2)], axis=1
    ).astype(BF16)

    def query_operand(whole, ws):
        turned = whole[...].astype(F32).T.astype(BF16)
        for h in range(4):
            cols = pl.ds(h * CHIP, CHIP)
            ws[0:64, cols] = turned[h * 64:(h + 1) * 64, :]
            ws[64:128, cols] = jnp.zeros((64, CHIP), BF16)
            ws[128:256, cols] = one_hot

    gather_b.step2()
    halves(dot(nb[...], wq[...], NN) * 0.125, qst_f, qxf)
    m_qf.start()
    m_qb.wait_recv()
    query_operand(qxb, ws_b)
    gather_b.step3()
    m_do.wait_recv()
    turned = dox[...].astype(F32).T.astype(BF16)
    nothing = jnp.zeros((CHIP, 64), F32)
    for h in range(4):
        cols = pl.ds(h * CHIP, CHIP)
        wd[0:64, cols] = jnp.zeros((64, CHIP), BF16)
        wd[64:128, cols] = turned[h * 64:(h + 1) * 64, :]
        head_q = qxb[:, h * 64:(h + 1) * 64].astype(F32)
        head_o = dox[:, h * 64:(h + 1) * 64].astype(F32)
        wkq[cols, :] = jnp.concatenate([head_q, nothing], axis=1).astype(BF16)
        wvo[cols, :] = jnp.concatenate([nothing, head_o], axis=1).astype(BF16)
    gather_b.step4()
    m_kvf.wait_recv()
    gather_f.start()
    m_qf.wait_recv()
    query_operand(qxf, ws_f)

    PS, SS = (pa, pb), (sa, sb)

    def keys_of(kv, block):
        pos, half = block
        return kv[pos, 2 * half:2 * half + 2].reshape(KB, 128)

    def attention(kv, ws, hooks):
        acc[...] = jnp.zeros_like(acc)
        maxima = []
        lane = lax.broadcasted_iota(jnp.int32, (KB, 128), 1)
        for t in range(10):
            if t in hooks:
                hooks[t]()
            if t < 8:
                operand = jnp.concatenate(
                    [keys_of(kv, FORWARD_ORDER[t]), keys_of(aux, FORWARD_ORDER[t])], axis=1
                )
                tops = []
                for r in range(4):
                    cols = pl.ds(r * CHIP, CHIP)
                    scores = dot(operand, ws[:, cols], NN)
                    SS[t % 2][:, cols] = scores
                    tops.append(jnp.max(scores.reshape(KB // 8, 8, CHIP), axis=0))
                top = jnp.max(jnp.concatenate(tops, axis=1), axis=0, keepdims=True)
                before = maxima[-1] if maxima else jnp.full((1, QROWS), FIRST_MAX, F32)
                maxima.append(jnp.maximum(before, top))
                mrow[t:t + 1, :] = maxima[-1]
            if 1 <= t <= 8:
                n = t - 1
                for r in range(4):
                    cols = pl.ds(r * CHIP, CHIP)
                    PS[n % 2][n // 2, :, cols] = jnp.exp(
                        SS[n % 2][:, cols] - maxima[n][:, r * CHIP:(r + 1) * CHIP]
                    ).astype(BF16)
            if t >= 2:
                n = t - 2
                block = keys_of(kv, FORWARD_ORDER[n])
                turned = jnp.where(lane < 64, jnp.ones_like(block), block).T
                term = dot(turned, PS[n % 2][n // 2], NN)
                if n == 0:
                    acc[...] = term
                else:
                    acc[...] = acc[...] * jnp.exp(maxima[n - 1] - maxima[n]) + term
        return maxima[-1]

    def tokens_first(columns, staged, whole):
        tall = jnp.concatenate([columns[:, h * CHIP:(h + 1) * CHIP] for h in range(4)], axis=0)
        rows = tall.T.astype(BF16)
        staged[0] = rows[0:128]
        staged[1] = rows[128:256]
        whole[core] = staged[core]

    def wait_x2():
        gather_b.x2[0].wait_recv()
        gather_b.x2[1].wait_recv()

    final_max = attention(
        kvb, ws_b, {2: gather_f.step1, 4: gather_f.step2, 6: wait_x2}
    )
    inverse_sum = 1.0 / acc[0:1, :]
    attended = (acc[64:128, :] * inverse_sum).astype(BF16).astype(F32)
    delta = jnp.sum(wd[64:128, :].astype(F32) * attended, axis=0, keepdims=True)
    frow[...] = jnp.exp(mrow[...] - final_max) * inverse_sum

    TS, US = (ta, tb), (ua, ub)
    accq[...] = jnp.zeros_like(accq)

    for t in range(9):
        if t == 1:
            gather_f.step3()
        if t == 3:
            gather_f.step4()
        if t < 8:
            n = FORWARD_ORDER.index(BACKWARD_ORDER[t])
            keys = keys_of(kvb, BACKWARD_ORDER[t])
            for r in range(4):
                cols = pl.ds(r * CHIP, CHIP)
                grads = dot(keys, wd[:, cols], NN) - delta[:, r * CHIP:(r + 1) * CHIP]
                prob = PS[n % 2][n // 2, :, cols].astype(F32) * frow[n:n + 1, cols]
                TS[t % 2][:, cols] = prob.astype(BF16)
                US[t % 2][:, cols] = (prob * grads).astype(BF16)
        if t >= 1:
            pos, half = BACKWARD_ORDER[t - 1]
            score_grads = US[(t - 1) % 2][...]
            accq[...] += dot(keys_of(kvb, (pos, half)).T, score_grads, NN)
            terms = dot(score_grads, wkq[...], NN) + dot(TS[(t - 1) % 2][...], wvo[...], NN)
            terms = terms.reshape(2, CHIP, 128)
            if (pos, half) == (1, 0):
                r_half[0].wait_recv()
                terms = terms + rxh[0].astype(F32)
            if (pos, half) == (2, 1):
                r_half[1].wait_recv()
                terms = terms + rxh[1].astype(F32)
            if pos == 0:
                d0[2 * half:2 * half + 2] = terms
            else:
                dkv[pos, 2 * half:2 * half + 2] = terms.astype(BF16)
                (r_half[half] if pos == 3 else r_full[(pos, half)]).start()

    tokens_first(accq[0:64, :] * 0.125, dqst, dqx)
    m_dq.start()

    def sum_x():
        for half in range(2):
            r_full[(1, half)].wait_recv()
            r_full[(2, half)].wait_recv()
            whole = (
                d0[2 * half:2 * half + 2] + rxf[0, half].astype(F32) + rxf[1, half].astype(F32)
            )
            d0[2 * half:2 * half + 2] = whole
        dkv[0, 2] = d0[2].astype(BF16)
        ry_half[0].start()
        ry_half[1].start()

    def sum_y():
        ry_half[0].wait_recv()
        dkv[0, 1, 0:128] = (d0[1, 0:128] + ryh[0].astype(F32)).astype(BF16)
        dkv[0, 1, 128:256] = d0[1, 128:256].astype(BF16)
        ry_full[0].start()
        ry_half[1].wait_recv()
        dkv[0, 3, 0:128] = d0[3, 0:128].astype(BF16)
        dkv[0, 3, 128:256] = (d0[3, 128:256] + ryh[1].astype(F32)).astype(BF16)
        ry_full[1].start()

    def sum_own():
        ry_full[0].wait_recv()
        ry_full[1].wait_recv()
        whole = (d0[0] + ryf[0].astype(F32) + ryf[1].astype(F32)).astype(BF16)
        dfst[0] = whole[0:128]
        dfst[1] = whole[128:256]
        dfin[core] = dfst[core]
        m_dkv.start()

    def finish_backward():
        m_dq.wait_recv()
        m_dkv.wait_recv()
        first, second = dfin[0].astype(F32), dfin[1].astype(F32)
        key_value = jnp.concatenate(
            [first[:, 0:64], second[:, 0:64], first[:, 64:128], second[:, 64:128]], axis=1
        ).astype(BF16)
        grads = dot(jnp.concatenate([dqx[0], dqx[1]], axis=1), wq[...], NT)
        grads = grads + dot(key_value, wkv[...], NT)
        scaled = grads * gain[...]
        wide = xb[...].astype(F32)
        inverse = lax.rsqrt(jnp.mean(wide * wide, axis=-1, keepdims=True) + NORM_EPSILON)
        mean = jnp.mean(wide * scaled, axis=-1, keepdims=True)
        stage_b[...] = (
            cot[...].astype(F32) + inverse * scaled - wide * (inverse * inverse * inverse) * mean
        ).astype(BF16)
        m_out_b.start()

    def wait_f():
        gather_f.x2[0].wait_recv()
        gather_f.x2[1].wait_recv()

    def hook6():
        wait_f()
        sum_own()

    attention(kvf, ws_f, {2: sum_x, 4: sum_y, 6: hook6, 8: finish_backward})
    tokens_first(acc[64:128, :] * (1.0 / acc[0:1, :]), ost, att)
    m_att.start()
    m_att.wait_recv()
    stage_f[...] = (
        xf[...].astype(F32) + dot(jnp.concatenate([att[0], att[1]], axis=1), wo[...], NN)
    ).astype(BF16)
    m_out_f.start()
    for copy in used:
        copy.wait_send()
    m_out_b.wait_recv()
    m_out_f.wait_recv()


def on_device(
    forward_input, stored_input, output_cotangent, norm_gain,
    query_weight, key_weight, value_weight, output_weight, frame_index, valid_counts,
):
    any_space = pl.BlockSpec(memory_space=pl.ANY)
    vmem = pl.BlockSpec(memory_space=pltpu.VMEM)
    shape = jax.ShapeDtypeStruct((ROWS, D), BF16)
    scratch = [
        (ROWS, D), (ROWS, D), (ROWS, D), (D, 512), (D, 256), (512, D), (ROWS, D),
        (2, ROWS, 128), (2, ROWS, 128), (4, 4, CHIP, 128), (4, 4, CHIP, 128), (4, 4, CHIP, 128),
        (2, ROWS, 256), (2, ROWS, 256), (2, ROWS, 256), (CHIP, 256), (CHIP, 256), (CHIP, 256),
        (256, QROWS), (256, QROWS), (128, QROWS), (QROWS, 128), (QROWS, 128),
        (4, KB, QROWS), (4, KB, QROWS), ((KB, QROWS), F32), ((KB, QROWS), F32),
        (KB, QROWS), (KB, QROWS), (KB, QROWS), (KB, QROWS),
        ((128, QROWS), F32), ((128, QROWS), F32), ((8, QROWS), F32), ((8, QROWS), F32),
        (4, 4, CHIP, 128), ((4, CHIP, 128), F32), (2, 2, CHIP, 128), (2, 2, 2, CHIP, 128),
        (2, ROWS, 128), (2, CHIP, 128), (2, ROWS, 128), (2, ROWS, 128),
        (2, ROWS, 256), (2, ROWS, 256), (2, ROWS, 256), (2, ROWS, 256), (ROWS, D), (ROWS, D),
    ]
    scratch = [
        pltpu.VMEM(*s) if isinstance(s[1], type) or not isinstance(s[1], int) else pltpu.VMEM(s, BF16)
        for s in scratch
    ]
    out_f, out_b = pl.pallas_call(
        fused,
        out_shape=(shape, shape),
        in_specs=[any_space] * 3 + [vmem] + [any_space] * 4
        + [vmem, pl.BlockSpec(memory_space=pltpu.SMEM)],
        out_specs=(any_space, any_space),
        scratch_shapes=scratch + [
            pltpu.SemaphoreType.DMA((7,)),
            pltpu.SemaphoreType.DMA((MESSAGES,)),
            pltpu.SemaphoreType.DMA((MESSAGES,)),
        ],
        compiler_params=pltpu.CompilerParams(
            collective_id=0, has_side_effects=True, vmem_limit_bytes=56 * 2**20
        ),
        name="sublayer",
    )(
        forward_input[0], stored_input[0], output_cotangent[0], norm_gain,
        query_weight[0], key_weight[0], value_weight[0], output_weight[0],
        frame_index.reshape(32, 128), valid_counts,
    )
    return out_f[None], out_b[None]


def solution(mesh):
    return jax.shard_map(
        on_device,
        mesh=mesh,
        in_specs=(
            P("section", "seq", None),
            P("section", "seq", None),
            P("section", "seq", None),
            P("section", None),
            P("section", None, None),
            P("section", None, None),
            P("section", None, None),
            P("section", None, None),
            P(),
            P(),
        ),
        out_specs=(P("section", "seq", None), P("section", "seq", None)),
        check_vma=False,
    )
```

time: 446 us -> 84.9 us (0.19)
  waiting for transfers between devices: 281 us -> 0 us
  Pallas kernels: 0 us -> 81.3 us
  local copies, waits for them, and re-layouts: 68.9 us -> 2.42 us
  loops' own time: 47 us -> 0 us
  matrix products: 16.4 us -> 0 us
  between operations: 14.2 us -> 0.65 us
  starting transfers between devices: 7.71 us -> 0 us
  other arithmetic: 7.43 us -> 0 us
    reduce_scatter x2 -> x0, waiting for transfers between devices: 215 us -> none  [on_device(): lax.psum_scatter(key_value_terms, 'seq', scatter_dimension=0, tiled=True)]
    pallas_call x0 -> x1, Pallas kernels: none -> 81.3 us  [on_device(): pl.pallas_call(fused, out_shape=(shape, shape), in_specs=[any_space] * 3...]
    all_gather x2 -> x0, waiting for transfers between devices: 62.8 us -> none  [side_by_side(): lax.all_gather(both, axis, axis=dim, tiled=True)]
    another operation x27 -> x0, loops' own time: 47 us -> none  [the longest x2 30.9 us: fold_blocks(): lax.scan(fold_advance, carried, (jnp.arange(blocks, dtype=jnp.int32), sta...]
    dynamic_slice x57 -> x0, local copies, waits for them, and re-layouts: 31.7 us -> none  [the longest x26 16 us: fold_blocks(): lax.scan(fold_advance, carried, (jnp.arange(blocks, dtype=jnp.int32), sta...]
    slice x26 -> x0, local copies, waits for them, and re-layouts: 18.1 us -> none  [the longest x16 9.62 us: attend(): beyond = frame_index[first_row] > query_frames[-1]]
    dot_general x20 -> x0, matrix products: 16.4 us -> none  [the longest x6 5.21 us: project(): jnp.dot(normed, weight, preferred_element_type=jnp.float32)]
    dynamic_update_slice x24 -> x0, local copies, waits for them, and re-layouts: 8.77 us -> none  [local_backward(): lax.scan(local_advance, start_grad, (jnp.arange(blocks, dtype=jnp.int32),...]
  transfers between devices with their start and end apart: 6 -> 0, of which waited for: 4 -> 0; matrix products, arithmetic and copies ran while one was open for 20% -> 0% of each run, Pallas kernels for 0% -> 0%
where the time goes in v1:
time: 84.9 us; the launch traced here: 84.4 us
  Pallas kernels  81.3 us (96%)
  local copies, waits for them, and re-layouts  2.42 us (3%)
    pallas_call x1, Pallas kernels, on_device(): pl.pallas_call(fused, out_shape=(shape, shape), in_specs=[any_space] * 3...  81.3 us
    unnamed x4, local copies, waits for them, and re-layouts  2.42 us

profile of v1, /device:TPU:1, one launch (start us, length us, event | category | flops | bytes accessed | tf_op | source)
XLA Modules:
  0.0 84.4 jit_solution(12350883849135750777)
XLA Ops:
  0.6 81.3 %sublayer.1 = (bf16[128,1024]{1,0:T(8,128)(2,1)}, bf16[128,1024]{1,0:T(8,128)(2,1)}) custom-call(bf16[128,1024]{1,0:T(8,128)(2,1)} %bitcast.12, bf16[128,1024]{1,0:T(8,128)(2,1)} %bitcast.13, bf16[128,1024]{1,0:T(8,128)(2,1)} %bitcast.14, f32[1,1024]{1,0:T(1,128)} %gain.1, bf16[1024,512]{1,0:T(8,128)(2,1)} %bitcast.10, bf16[1024,128]{1,0:T(8,128)(2,1)} %bitcast.15, ...), custom_call_target="tpu_custom_call" | custom-call | tf_op jit(solution)/shard_map/sublayer/pallas_call | solution.py:451
  82.0 0.0 copy-start
  82.0 1.7 %copy.14 = bf16[1,128,1024]{2,1,0:T(8,128)(2,1)} copy(bf16[1,128,1024]{2,1,0:T(8,128)(2,1)} %bitcast.18) | data formatting | bytes 524288
  83.7 0.0 copy-done
  83.7 0.7 copy.15
Async XLA Ops:
  82.0 1.7 %copy-start = (bf16[128,1024]{1,0:T(8,128)(2,1)S(1)}, bf16[128,1024]{1,0:T(8,128)(2,1)}, u32[]{:S(2)}) copy-start(bf16[128,1024]{1,0:T(8,128)(2,1)} %get-tuple-element.5) | copy-start | bytes 786436

commit v2 on v1

--- a/solution.py
+++ b/solution.py
@@ -1,6 +1,3 @@
-import functools
-import math
-
 import jax
 import jax.numpy as jnp
 from jax import lax
@@ -22,10 +19,9 @@
 NN = (((1,), (0,)), ((), ()))
 NT = (((1,), (1,)), ((), ()))
 
-OFFSET_X = (0, 1, 3, 2)
-FORWARD_ORDER = ((0, 0), (0, 1), (1, 0), (2, 0), (1, 1), (2, 1), (3, 0), (3, 1))
-BACKWARD_ORDER = ((3, 0), (3, 1), (1, 1), (2, 0), (1, 0), (2, 1), (0, 0), (0, 1))
-MESSAGES = 40
+FORWARD_ORDER = ((0, 0), (0, 1), (1, 0), (3, 0), (2, 0), (2, 1), (1, 1), (3, 1))
+BACKWARD_ORDER = ((2, 1), (2, 0), (1, 1), (1, 0), (3, 1), (3, 0), (0, 1), (0, 0))
+MESSAGES = 61
 
 
 def dot(a, b, dims):
@@ -41,7 +37,7 @@
     ws_b, ws_f, wd, wkq, wvo,
     pa, pb, sa, sb, ta, tb, ua, ub,
     acc, accq, mrow, frow,
-    dkv, d0, rxh, rxf, ryh, ryf, dfst, dfin,
+    dkv, d0, rx, ry, dfst, dfin, part,
     ost, att, dqst, dqx, stage_f, stage_b,
     load_sem, send_sem, recv_sem,
 ):
@@ -57,6 +53,7 @@
     partner = at(x, yh, other)
     xp, xm = at((x + 1) % 4, yh, core), at((x + 3) % 4, yh, core)
     yp, ym = at(x, (yh + 1) % 4, core), at(x, (yh + 3) % 4, core)
+    x2, y2 = at((x + 2) % 4, yh, core), at(x, (yh + 2) % 4, core)
     sp, sm = {"section": (sec + 1) % n_sec}, {"section": (sec + n_sec - 1) % n_sec}
 
     loads = []
@@ -69,7 +66,7 @@
         loads.append(copy)
 
     barrier = pltpu.get_barrier_semaphore()
-    for dev in (partner, xp, xm, yp, ym, sp, sm):
+    for dev in (partner, xp, xm, x2, yp, ym, y2, sp, sm):
         pl.semaphore_signal(barrier, inc=1, device_id=dev, device_id_type=pl.DeviceIdType.MESH)
 
     used = []
@@ -96,63 +93,64 @@
 
     class Gather:
         def __init__(self, kv):
-            self.y = (message(kv.at[0, 0], kv.at[0, 3], yp), message(kv.at[0, 0], kv.at[0, 1], ym))
-            self.y2 = (
-                message(kv.at[0, 3, 0:128], kv.at[0, 2, 0:128], yp),
-                message(kv.at[0, 1, 128:256], kv.at[0, 2, 128:256], ym),
+            own = kv.at[0, 0]
+            self.y = (
+                message(own, kv.at[3, 0], yp), message(own, kv.at[1, 0], ym),
+                message(own, kv.at[2, 0], y2),
             )
             self.x = tuple(
-                (
-                    message(kv.at[0, 2 * h:2 * h + 2], kv.at[2, 2 * h:2 * h + 2], xp),
-                    message(kv.at[0, 2 * h:2 * h + 2], kv.at[1, 2 * h:2 * h + 2], xm),
+                (message(kv.at[d, 0], kv.at[d, 2], xp), message(kv.at[d, 0], kv.at[d, 1], xm))
+                for d in range(4)
+            )
+            self.far = {
+                d: (
+                    message(kv.at[d, 2, 0:128], kv.at[d, 3, 0:128], xp),
+                    message(kv.at[d, 1, 128:256], kv.at[d, 3, 128:256], xm),
                 )
-                for h in range(2)
-            )
-            self.x2 = (
-                message(kv.at[2, 0:2], kv.at[3, 0:2], xp),
-                message(kv.at[1, 2:4], kv.at[3, 2:4], xm),
-            )
-
-        def start(self):
-            self.y[0].start()
-            self.y[1].start()
-
-        def step1(self):
+                for d in (0, 1, 3)
+            }
+            self.far[2] = (message(kv.at[2, 0], kv.at[2, 3], x2),)
+
+        def start_y(self):
+            for copy in self.y:
+                copy.start()
+
+        def start_x(self, d):
+            for copy in self.x[d]:
+                copy.start()
+
+        def near(self):
             self.y[0].wait_recv()
+            self.start_x(3)
             self.y[1].wait_recv()
-            self.y2[0].start()
-            self.y2[1].start()
-            self.x[0][0].start()
-            self.x[0][1].start()
-
-        def step2(self):
-            self.y2[0].wait_recv()
-            self.y2[1].wait_recv()
-            self.x[1][0].start()
-            self.x[1][1].start()
-
-        def step3(self):
-            self.x[0][0].wait_recv()
-            self.x2[0].start()
-            self.x[0][1].wait_recv()
-
-        def step4(self):
-            self.x[1][1].wait_recv()
-            self.x2[1].start()
-            self.x[1][0].wait_recv()
+            self.start_x(1)
+
+        def middle(self):
+            self.y[2].wait_recv()
+            self.start_x(2)
+            self.far[2][0].start()
+
+        def forward(self, d):
+            self.x[d][0].wait_recv()
+            self.far[d][0].start()
+            self.x[d][1].wait_recv()
+            self.far[d][1].start()
+
+        def wait_x(self, d):
+            for copy in self.x[d]:
+                copy.wait_recv()
+
+        def wait_far(self, d):
+            for copy in self.far[d]:
+                copy.wait_recv()
 
     gather_b, gather_f = Gather(kvb), Gather(kvf)
 
-    r_half = (message(dkv.at[3, 0:2], rxh.at[0], xp), message(dkv.at[3, 2:4], rxh.at[1], xm))
-    r_full = {
-        (1, h): message(dkv.at[1, 2 * h:2 * h + 2], rxf.at[0, h], xp) for h in range(2)
-    } | {
-        (2, h): message(dkv.at[2, 2 * h:2 * h + 2], rxf.at[1, h], xm) for h in range(2)
+    sum_x = {
+        (d, p): message(dkv.at[d, p], rx.at[d, p - 1], dev)
+        for d in range(4) for p, dev in ((1, xp), (2, xm), (3, x2))
     }
-    ry_half = (
-        message(dkv.at[0, 2, 0:128], ryh.at[0], yp), message(dkv.at[0, 2, 128:256], ryh.at[1], ym),
-    )
-    ry_full = (message(dkv.at[0, 1], ryf.at[0], yp), message(dkv.at[0, 3], ryf.at[1], ym))
+    sum_y = {d: message(dkv.at[d, 0], ry.at[d - 1], dev) for d, dev in ((1, yp), (2, y2), (3, ym))}
 
     m_out_f = message(stage_f, out_f, sp)
     m_out_b = message(stage_b, out_b, sm)
@@ -180,29 +178,30 @@
     loads[1].wait()
     loads[2].wait()
     key_values(nb[...], kvst_b, kvb)
-    pl.semaphore_wait(barrier, 7)
+    pl.semaphore_wait(barrier, 9)
     m_kvb.start()
     loads[3].wait()
     halves(dot(nb[...], wq[...], NN) * 0.125, qst_b, qxb)
     m_qb.start()
     m_kvb.wait_recv()
-    gather_b.start()
+    gather_b.start_y()
+    gather_b.start_x(0)
     loads[4].wait()
     loads[5].wait()
     halves(dot(cot[...], wo[...], NT), dost, dox)
     m_do.start()
-    gather_b.step1()
 
     loads[6].wait()
     normed_f, _ = normalize(xf)
     nb[...] = normed_f
     key_values(nb[...], kvst_f, kvf)
     m_kvf.start()
+    gather_b.forward(0)
 
     chip = x * 4 + yh
 
     def mask_block(k, carry):
-        pos, dy = k // 4, k % 4
+        dy, pos = k // 4, k % 4
         dx = jnp.where(pos == 2, 3, jnp.where(pos == 3, 2, pos))
         chip_k = ((x + dx) % 4) * 4 + (yh + dy) % 4
         number = lax.broadcasted_iota(jnp.int32, (128, 128), 0)
@@ -211,7 +210,7 @@
             row = frames[pl.ds(2 * chip_k + h, 1), :]
             seen = (row <= number) & (lane < counts[2 * chip_k + h])
             bias = jnp.where(seen | (number >= 16), 0.0, MASKED)
-            aux[pos, dy, h * 128:(h + 1) * 128, :] = bias.T.astype(BF16)
+            aux[dy, pos, h * 128:(h + 1) * 128, :] = bias.T.astype(BF16)
         return carry
 
     lax.fori_loop(0, 16, mask_block, 0)
@@ -229,12 +228,15 @@
             ws[64:128, cols] = jnp.zeros((64, CHIP), BF16)
             ws[128:256, cols] = one_hot
 
-    gather_b.step2()
+    gather_b.near()
     halves(dot(nb[...], wq[...], NN) * 0.125, qst_f, qxf)
     m_qf.start()
     m_qb.wait_recv()
     query_operand(qxb, ws_b)
-    gather_b.step3()
+    gather_b.middle()
+    m_kvf.wait_recv()
+    gather_f.start_y()
+    gather_f.start_x(0)
     m_do.wait_recv()
     turned = dox[...].astype(F32).T.astype(BF16)
     nothing = jnp.zeros((CHIP, 64), F32)
@@ -246,17 +248,16 @@
         head_o = dox[:, h * 64:(h + 1) * 64].astype(F32)
         wkq[cols, :] = jnp.concatenate([head_q, nothing], axis=1).astype(BF16)
         wvo[cols, :] = jnp.concatenate([nothing, head_o], axis=1).astype(BF16)
-    gather_b.step4()
-    m_kvf.wait_recv()
-    gather_f.start()
+    gather_b.forward(1)
+    gather_b.forward(3)
     m_qf.wait_recv()
     query_operand(qxf, ws_f)
 
     PS, SS = (pa, pb), (sa, sb)
 
     def keys_of(kv, block):
-        pos, half = block
-        return kv[pos, 2 * half:2 * half + 2].reshape(KB, 128)
+        d, half = block
+        return kv[d, 2 * half:2 * half + 2].reshape(KB, 128)
 
     def attention(kv, ws, hooks):
         acc[...] = jnp.zeros_like(acc)
@@ -304,26 +305,49 @@
         staged[1] = rows[128:256]
         whole[core] = staged[core]
 
-    def wait_x2():
-        gather_b.x2[0].wait_recv()
-        gather_b.x2[1].wait_recv()
+    def last_f():
+        gather_b.wait_far(1)
+        gather_f.near()
+
+    def middle_f():
+        gather_b.wait_far(3)
+        gather_f.middle()
 
     final_max = attention(
-        kvb, ws_b, {2: gather_f.step1, 4: gather_f.step2, 6: wait_x2}
+        kvb, ws_b,
+        {
+            1: lambda: gather_b.wait_far(0),
+            2: lambda: gather_f.forward(0),
+            4: lambda: gather_b.wait_x(2),
+            5: lambda: gather_b.wait_far(2),
+            6: last_f,
+            7: middle_f,
+        },
     )
     inverse_sum = 1.0 / acc[0:1, :]
     attended = (acc[64:128, :] * inverse_sum).astype(BF16).astype(F32)
     delta = jnp.sum(wd[64:128, :].astype(F32) * attended, axis=0, keepdims=True)
     frow[...] = jnp.exp(mrow[...] - final_max) * inverse_sum
 
+    def add_x(d):
+        whole = d0[d]
+        for p in (1, 2, 3):
+            sum_x[(d, p)].wait_recv()
+            whole = whole + rx[d, p - 1].astype(F32)
+        dkv[d, 0] = whole.astype(BF16)
+        sum_y[d].start()
+
     TS, US = (ta, tb), (ua, ub)
     accq[...] = jnp.zeros_like(accq)
 
     for t in range(9):
-        if t == 1:
-            gather_f.step3()
         if t == 3:
-            gather_f.step4()
+            gather_f.forward(1)
+        if t == 4:
+            gather_f.forward(3)
+        if t == 8:
+            gather_f.wait_x(2)
+            add_x(2)
         if t < 8:
             n = FORWARD_ORDER.index(BACKWARD_ORDER[t])
             keys = keys_of(kvb, BACKWARD_ORDER[t])
@@ -334,66 +358,48 @@
                 TS[t % 2][:, cols] = prob.astype(BF16)
                 US[t % 2][:, cols] = (prob * grads).astype(BF16)
         if t >= 1:
-            pos, half = BACKWARD_ORDER[t - 1]
+            d, half = BACKWARD_ORDER[t - 1]
             score_grads = US[(t - 1) % 2][...]
-            accq[...] += dot(keys_of(kvb, (pos, half)).T, score_grads, NN)
+            accq[...] += dot(keys_of(kvb, (d, half)).T, score_grads, NN)
             terms = dot(score_grads, wkq[...], NN) + dot(TS[(t - 1) % 2][...], wvo[...], NN)
-            terms = terms.reshape(2, CHIP, 128)
-            if (pos, half) == (1, 0):
-                r_half[0].wait_recv()
-                terms = terms + rxh[0].astype(F32)
-            if (pos, half) == (2, 1):
-                r_half[1].wait_recv()
-                terms = terms + rxh[1].astype(F32)
-            if pos == 0:
-                d0[2 * half:2 * half + 2] = terms
+            if half == 0:
+                d0[d] = terms[0:CHIP]
+                dkv[d, 1] = terms[CHIP:].astype(BF16)
+                sum_x[(d, 1)].start()
             else:
-                dkv[pos, 2 * half:2 * half + 2] = terms.astype(BF16)
-                (r_half[half] if pos == 3 else r_full[(pos, half)]).start()
+                dkv[d, 2] = terms[0:CHIP].astype(BF16)
+                dkv[d, 3] = terms[CHIP:].astype(BF16)
+                sum_x[(d, 3)].start()
+                sum_x[(d, 2)].start()
 
     tokens_first(accq[0:64, :] * 0.125, dqst, dqx)
     m_dq.start()
 
-    def sum_x():
-        for half in range(2):
-            r_full[(1, half)].wait_recv()
-            r_full[(2, half)].wait_recv()
-            whole = (
-                d0[2 * half:2 * half + 2] + rxf[0, half].astype(F32) + rxf[1, half].astype(F32)
-            )
-            d0[2 * half:2 * half + 2] = whole
-        dkv[0, 2] = d0[2].astype(BF16)
-        ry_half[0].start()
-        ry_half[1].start()
-
-    def sum_y():
-        ry_half[0].wait_recv()
-        dkv[0, 1, 0:128] = (d0[1, 0:128] + ryh[0].astype(F32)).astype(BF16)
-        dkv[0, 1, 128:256] = d0[1, 128:256].astype(BF16)
-        ry_full[0].start()
-        ry_half[1].wait_recv()
-        dkv[0, 3, 0:128] = d0[3, 0:128].astype(BF16)
-        dkv[0, 3, 128:256] = (d0[3, 128:256] + ryh[1].astype(F32)).astype(BF16)
-        ry_full[1].start()
+    def query_part():
+        m_dq.wait_recv()
+        part[...] = dot(jnp.concatenate([dqx[0], dqx[1]], axis=1), wq[...], NT)
 
     def sum_own():
-        ry_full[0].wait_recv()
-        ry_full[1].wait_recv()
-        whole = (d0[0] + ryf[0].astype(F32) + ryf[1].astype(F32)).astype(BF16)
+        whole = d0[0]
+        for p in (1, 2, 3):
+            sum_x[(0, p)].wait_recv()
+            whole = whole + rx[0, p - 1].astype(F32)
+        for d in (1, 3, 2):
+            sum_y[d].wait_recv()
+            whole = whole + ry[d - 1].astype(F32)
+        whole = whole.astype(BF16)
         dfst[0] = whole[0:128]
         dfst[1] = whole[128:256]
         dfin[core] = dfst[core]
         m_dkv.start()
 
     def finish_backward():
-        m_dq.wait_recv()
         m_dkv.wait_recv()
         first, second = dfin[0].astype(F32), dfin[1].astype(F32)
         key_value = jnp.concatenate(
             [first[:, 0:64], second[:, 0:64], first[:, 64:128], second[:, 64:128]], axis=1
         ).astype(BF16)
-        grads = dot(jnp.concatenate([dqx[0], dqx[1]], axis=1), wq[...], NT)
-        grads = grads + dot(key_value, wkv[...], NT)
+        grads = part[...] + dot(key_value, wkv[...], NT)
         scaled = grads * gain[...]
         wide = xb[...].astype(F32)
         inverse = lax.rsqrt(jnp.mean(wide * wide, axis=-1, keepdims=True) + NORM_EPSILON)
@@ -403,26 +409,44 @@
         ).astype(BF16)
         m_out_b.start()
 
-    def wait_f():
-        gather_f.x2[0].wait_recv()
-        gather_f.x2[1].wait_recv()
-
-    def hook6():
-        wait_f()
-        sum_own()
-
-    attention(kvf, ws_f, {2: sum_x, 4: sum_y, 6: hook6, 8: finish_backward})
+    def ready_1():
+        gather_f.wait_far(1)
+        add_x(3)
+
+    attention(
+        kvf, ws_f,
+        {
+            1: lambda: gather_f.wait_far(0),
+            3: query_part,
+            4: lambda: add_x(1),
+            5: lambda: gather_f.wait_far(2),
+            6: ready_1,
+            7: lambda: gather_f.wait_far(3),
+        },
+    )
     tokens_first(acc[64:128, :] * (1.0 / acc[0:1, :]), ost, att)
     m_att.start()
+    sum_own()
     m_att.wait_recv()
     stage_f[...] = (
         xf[...].astype(F32) + dot(jnp.concatenate([att[0], att[1]], axis=1), wo[...], NN)
     ).astype(BF16)
     m_out_f.start()
+    finish_backward()
     for copy in used:
         copy.wait_send()
     m_out_b.wait_recv()
     m_out_f.wait_recv()
+
+
+def hand_over(in_f, in_b, out_f, out_b, sem):
+    copies = [
+        pltpu.make_async_copy(in_f, out_f, sem.at[0]), pltpu.make_async_copy(in_b, out_b, sem.at[1]),
+    ]
+    for copy in copies:
+        copy.start()
+    for copy in copies:
+        copy.wait()
 
 
 def on_device(
@@ -440,8 +464,8 @@
         (4, KB, QROWS), (4, KB, QROWS), ((KB, QROWS), F32), ((KB, QROWS), F32),
         (KB, QROWS), (KB, QROWS), (KB, QROWS), (KB, QROWS),
         ((128, QROWS), F32), ((128, QROWS), F32), ((8, QROWS), F32), ((8, QROWS), F32),
-        (4, 4, CHIP, 128), ((4, CHIP, 128), F32), (2, 2, CHIP, 128), (2, 2, 2, CHIP, 128),
-        (2, ROWS, 128), (2, CHIP, 128), (2, ROWS, 128), (2, ROWS, 128),
+        (4, 4, CHIP, 128), ((4, CHIP, 128), F32), (4, 3, CHIP, 128), (3, CHIP, 128),
+        (2, ROWS, 128), (2, ROWS, 128), ((ROWS, D), F32),
         (2, ROWS, 256), (2, ROWS, 256), (2, ROWS, 256), (2, ROWS, 256), (ROWS, D), (ROWS, D),
     ]
     scratch = [
@@ -468,6 +492,14 @@
         query_weight[0], key_weight[0], value_weight[0], output_weight[0],
         frame_index.reshape(32, 128), valid_counts,
     )
+    out_f, out_b = pl.pallas_call(
+        hand_over,
+        out_shape=(shape, shape),
+        in_specs=[any_space] * 2,
+        out_specs=(any_space, any_space),
+        scratch_shapes=[pltpu.SemaphoreType.DMA((2,))],
+        name="hand_over",
+    )(out_f, out_b)
     return out_f[None], out_b[None]
 
 

time: 84.9 us -> 91.9 us (1.082); the launches traced: 84.4 us -> 90.3 us
  Pallas kernels: 81.3 us -> 89.5 us
  local copies, waits for them, and re-layouts: 2.42 us -> 0 us
    pallas_call x0 -> x1, Pallas kernels: none -> 17 us  [on_device(): pl.pallas_call(hand_over, out_shape=(shape, shape), in_specs=[any_space]...]
    pallas_call x1, Pallas kernels: 81.3 us -> 72.5 us  [on_device(): pl.pallas_call(fused, out_shape=(shape, shape), in_specs=[any_space] * 3...]
    unnamed x4 -> x0, local copies, waits for them, and re-layouts: 2.42 us -> none
where the time goes in v2:
time: 91.9 us; the launch traced here: 90.3 us
  Pallas kernels  89.5 us (97%)
    pallas_call x1, Pallas kernels, on_device(): pl.pallas_call(fused, out_shape=(shape, shape), in_specs=[any_space] * 3...  72.5 us
    pallas_call x1, Pallas kernels, on_device(): pl.pallas_call(hand_over, out_shape=(shape, shape), in_specs=[any_space]...  17 us

profile of v2, /device:TPU:1, one launch (start us, length us, event | category | flops | bytes accessed | tf_op | source)
XLA Modules:
  0.0 90.3 jit_solution(4436988068923366743)
XLA Ops:
  0.6 72.5 %sublayer.1 = (bf16[128,1024]{1,0:T(8,128)(2,1)}, bf16[128,1024]{1,0:T(8,128)(2,1)}) custom-call(bf16[128,1024]{1,0:T(8,128)(2,1)} %bitcast.12, bf16[128,1024]{1,0:T(8,128)(2,1)} %bitcast.13, bf16[128,1024]{1,0:T(8,128)(2,1)} %bitcast.14, f32[1,1024]{1,0:T(1,128)} %gain.1, bf16[1024,512]{1,0:T(8,128)(2,1)} %bitcast.10, bf16[1024,128]{1,0:T(8,128)(2,1)} %bitcast.15, ...), custom_call_target="tpu_custom_call" | custom-call | tf_op jit(solution)/shard_map/sublayer/pallas_call | solution.py:475
  73.2 17.0 %hand_over.1 = (bf16[128,1024]{1,0:T(8,128)(2,1)}, bf16[128,1024]{1,0:T(8,128)(2,1)}) custom-call(bf16[128,1024]{1,0:T(8,128)(2,1)} %get-tuple-element.6.in_f, bf16[128,1024]{1,0:T(8,128)(2,1)} %get-tuple-element.7.in_b), custom_call_target="tpu_custom_call" | custom-call | tf_op jit(solution)/shard_map/hand_over/pallas_call | solution.py:495

commit v3 on v2

--- a/solution.py
+++ b/solution.py
@@ -186,17 +186,16 @@
     m_kvb.wait_recv()
     gather_b.start_y()
     gather_b.start_x(0)
-    loads[4].wait()
-    loads[5].wait()
-    halves(dot(cot[...], wo[...], NT), dost, dox)
-    m_do.start()
 
     loads[6].wait()
     normed_f, _ = normalize(xf)
     nb[...] = normed_f
     key_values(nb[...], kvst_f, kvf)
     m_kvf.start()
-    gather_b.forward(0)
+    loads[4].wait()
+    loads[5].wait()
+    halves(dot(cot[...], wo[...], NT), dost, dox)
+    m_do.start()
 
     chip = x * 4 + yh
 
@@ -228,15 +227,15 @@
             ws[64:128, cols] = jnp.zeros((64, CHIP), BF16)
             ws[128:256, cols] = one_hot
 
-    gather_b.near()
+    m_qb.wait_recv()
+    query_operand(qxb, ws_b)
+    gather_b.forward(0)
+    m_kvf.wait_recv()
+    gather_f.start_x(0)
     halves(dot(nb[...], wq[...], NN) * 0.125, qst_f, qxf)
     m_qf.start()
-    m_qb.wait_recv()
-    query_operand(qxb, ws_b)
-    gather_b.middle()
-    m_kvf.wait_recv()
+    gather_b.near()
     gather_f.start_y()
-    gather_f.start_x(0)
     m_do.wait_recv()
     turned = dox[...].astype(F32).T.astype(BF16)
     nothing = jnp.zeros((CHIP, 64), F32)
@@ -248,8 +247,6 @@
         head_o = dox[:, h * 64:(h + 1) * 64].astype(F32)
         wkq[cols, :] = jnp.concatenate([head_q, nothing], axis=1).astype(BF16)
         wvo[cols, :] = jnp.concatenate([nothing, head_o], axis=1).astype(BF16)
-    gather_b.forward(1)
-    gather_b.forward(3)
     m_qf.wait_recv()
     query_operand(qxf, ws_f)
 
@@ -305,23 +302,26 @@
         staged[1] = rows[128:256]
         whole[core] = staged[core]
 
-    def last_f():
+    def second_row():
+        gather_b.middle()
+        gather_b.forward(1)
+        gather_f.forward(0)
+
+    def last_b():
         gather_b.wait_far(1)
         gather_f.near()
-
-    def middle_f():
-        gather_b.wait_far(3)
-        gather_f.middle()
 
     final_max = attention(
         kvb, ws_b,
         {
             1: lambda: gather_b.wait_far(0),
-            2: lambda: gather_f.forward(0),
+            2: second_row,
+            3: lambda: gather_b.forward(3),
             4: lambda: gather_b.wait_x(2),
             5: lambda: gather_b.wait_far(2),
-            6: last_f,
-            7: middle_f,
+            6: last_b,
+            7: lambda: gather_b.wait_far(3),
+            8: gather_f.middle,
         },
     )
     inverse_sum = 1.0 / acc[0:1, :]
@@ -341,12 +341,11 @@
     accq[...] = jnp.zeros_like(accq)
 
     for t in range(9):
-        if t == 3:
+        if t == 4:
             gather_f.forward(1)
-        if t == 4:
+        if t == 5:
             gather_f.forward(3)
         if t == 8:
-            gather_f.wait_x(2)
             add_x(2)
         if t < 8:
             n = FORWARD_ORDER.index(BACKWARD_ORDER[t])
@@ -379,11 +378,15 @@
         m_dq.wait_recv()
         part[...] = dot(jnp.concatenate([dqx[0], dqx[1]], axis=1), wq[...], NT)
 
-    def sum_own():
+    def add_own_x():
         whole = d0[0]
         for p in (1, 2, 3):
             sum_x[(0, p)].wait_recv()
             whole = whole + rx[0, p - 1].astype(F32)
+        d0[0] = whole
+
+    def sum_own():
+        whole = d0[0]
         for d in (1, 3, 2):
             sum_y[d].wait_recv()
             whole = whole + ry[d - 1].astype(F32)
@@ -409,29 +412,30 @@
         ).astype(BF16)
         m_out_b.start()
 
-    def ready_1():
-        gather_f.wait_far(1)
+    def fourth():
+        gather_f.wait_x(2)
         add_x(3)
 
     attention(
         kvf, ws_f,
         {
-            1: lambda: gather_f.wait_far(0),
+            1: lambda: (gather_f.wait_far(0), add_x(1)),
             3: query_part,
-            4: lambda: add_x(1),
+            4: fourth,
             5: lambda: gather_f.wait_far(2),
-            6: ready_1,
+            6: lambda: gather_f.wait_far(1),
             7: lambda: gather_f.wait_far(3),
+            9: add_own_x,
         },
     )
     tokens_first(acc[64:128, :] * (1.0 / acc[0:1, :]), ost, att)
     m_att.start()
-    sum_own()
     m_att.wait_recv()
     stage_f[...] = (
         xf[...].astype(F32) + dot(jnp.concatenate([att[0], att[1]], axis=1), wo[...], NN)
     ).astype(BF16)
     m_out_f.start()
+    sum_own()
     finish_backward()
     for copy in used:
         copy.wait_send()
@@ -439,14 +443,20 @@
     m_out_f.wait_recv()
 
 
-def hand_over(in_f, in_b, out_f, out_b, sem):
-    copies = [
-        pltpu.make_async_copy(in_f, out_f, sem.at[0]), pltpu.make_async_copy(in_b, out_b, sem.at[1]),
-    ]
-    for copy in copies:
-        copy.start()
-    for copy in copies:
-        copy.wait()
+def hand_over(in_f, in_b, out_f, out_b, held, in_sem, out_sem):
+    pieces = []
+    for i, (src, dst) in enumerate(((in_f, out_f), (in_b, out_b))):
+        for h in range(2):
+            rows = pl.ds(64 * h, 64)
+            arrive = pltpu.make_async_copy(src.at[rows], held.at[i, rows], in_sem.at[2 * i + h])
+            leave = pltpu.make_async_copy(held.at[i, rows], dst.at[rows], out_sem.at[2 * i + h])
+            arrive.start()
+            pieces.append((arrive, leave))
+    for arrive, leave in pieces:
+        arrive.wait()
+        leave.start()
+    for _, leave in pieces:
+        leave.wait()
 
 
 def on_device(
@@ -497,7 +507,9 @@
         out_shape=(shape, shape),
         in_specs=[any_space] * 2,
         out_specs=(any_space, any_space),
-        scratch_shapes=[pltpu.SemaphoreType.DMA((2,))],
+        scratch_shapes=[
+            pltpu.VMEM((2, ROWS, D), BF16), pltpu.SemaphoreType.DMA((4,)), pltpu.SemaphoreType.DMA((4,)),
+        ],
         name="hand_over",
     )(out_f, out_b)
     return out_f[None], out_b[None]

time: 91.9 us -> 74.4 us (0.81); the launches traced: 90.3 us -> 74.2 us
  Pallas kernels: 89.5 us -> 73.4 us
    pallas_call x1, Pallas kernels: 17 us -> 1.82 us  [on_device(): pl.pallas_call(hand_over, out_shape=(shape, shape), in_specs=[any_space]...]
    pallas_call x1, Pallas kernels: 72.5 us -> 71.6 us  [on_device(): pl.pallas_call(fused, out_shape=(shape, shape), in_specs=[any_space] * 3...]
where the time goes in v3:
time: 74.4 us; the launch traced here: 74.2 us
  Pallas kernels  73.4 us (99%)
  between operations  0.8 us (1%)
    pallas_call x1, Pallas kernels, on_device(): pl.pallas_call(fused, out_shape=(shape, shape), in_specs=[any_space] * 3...  71.6 us
    pallas_call x1, Pallas kernels, on_device(): pl.pallas_call(hand_over, out_shape=(shape, shape), in_specs=[any_space]...  1.82 us

profile of v3, /device:TPU:1, one launch (start us, length us, event | category | flops | bytes accessed | tf_op | source)
XLA Modules:
  0.0 74.2 jit_solution(9102128905317397958)
XLA Ops:
  0.6 71.6 %sublayer.1 = (bf16[128,1024]{1,0:T(8,128)(2,1)}, bf16[128,1024]{1,0:T(8,128)(2,1)}) custom-call(bf16[128,1024]{1,0:T(8,128)(2,1)} %bitcast.12, bf16[128,1024]{1,0:T(8,128)(2,1)} %bitcast.13, bf16[128,1024]{1,0:T(8,128)(2,1)} %bitcast.14, f32[1,1024]{1,0:T(1,128)} %gain.1, bf16[1024,512]{1,0:T(8,128)(2,1)} %bitcast.10, bf16[1024,128]{1,0:T(8,128)(2,1)} %bitcast.15, ...), custom_call_target="tpu_custom_call" | custom-call | tf_op jit(solution)/shard_map/sublayer/pallas_call | solution.py:485
  72.2 1.8 %hand_over.1 = (bf16[128,1024]{1,0:T(8,128)(2,1)}, bf16[128,1024]{1,0:T(8,128)(2,1)}) custom-call(bf16[128,1024]{1,0:T(8,128)(2,1)} %get-tuple-element.6.in_f, bf16[128,1024]{1,0:T(8,128)(2,1)} %get-tuple-element.7.in_b), custom_call_target="tpu_custom_call" | custom-call | tf_op jit(solution)/shard_map/hand_over/pallas_call | solution.py:505

commit v4 on v3

--- a/solution.py
+++ b/solution.py
@@ -21,7 +21,7 @@
 
 FORWARD_ORDER = ((0, 0), (0, 1), (1, 0), (3, 0), (2, 0), (2, 1), (1, 1), (3, 1))
 BACKWARD_ORDER = ((2, 1), (2, 0), (1, 1), (1, 0), (3, 1), (3, 0), (0, 1), (0, 0))
-MESSAGES = 61
+MESSAGES = 63
 
 
 def dot(a, b, dims):
@@ -152,8 +152,10 @@
     }
     sum_y = {d: message(dkv.at[d, 0], ry.at[d - 1], dev) for d, dev in ((1, yp), (2, y2), (3, ym))}
 
-    m_out_f = message(stage_f, out_f, sp)
-    m_out_b = message(stage_b, out_b, sm)
+    m_out_f = [
+        message(stage_f.at[:, c:c + 512], out_f.at[:, c:c + 512], sp) for c in (0, 512)
+    ]
+    m_out_b = [message(stage_b.at[r:r + 64], out_b.at[r:r + 64], sm) for r in (0, 64)]
     assert len(used) == MESSAGES
 
     def normalize(inputs):
@@ -307,8 +309,8 @@
         gather_b.forward(1)
         gather_f.forward(0)
 
-    def last_b():
-        gather_b.wait_far(1)
+    def third_row():
+        gather_b.forward(3)
         gather_f.near()
 
     final_max = attention(
@@ -316,12 +318,11 @@
         {
             1: lambda: gather_b.wait_far(0),
             2: second_row,
-            3: lambda: gather_b.forward(3),
+            3: third_row,
             4: lambda: gather_b.wait_x(2),
             5: lambda: gather_b.wait_far(2),
-            6: last_b,
+            6: lambda: (gather_b.wait_far(1), gather_f.middle()),
             7: lambda: gather_b.wait_far(3),
-            8: gather_f.middle,
         },
     )
     inverse_sum = 1.0 / acc[0:1, :]
@@ -341,9 +342,9 @@
     accq[...] = jnp.zeros_like(accq)
 
     for t in range(9):
-        if t == 4:
+        if t == 1:
             gather_f.forward(1)
-        if t == 5:
+        if t == 2:
             gather_f.forward(3)
         if t == 8:
             add_x(2)
@@ -402,15 +403,18 @@
         key_value = jnp.concatenate(
             [first[:, 0:64], second[:, 0:64], first[:, 64:128], second[:, 64:128]], axis=1
         ).astype(BF16)
-        grads = part[...] + dot(key_value, wkv[...], NT)
-        scaled = grads * gain[...]
-        wide = xb[...].astype(F32)
-        inverse = lax.rsqrt(jnp.mean(wide * wide, axis=-1, keepdims=True) + NORM_EPSILON)
-        mean = jnp.mean(wide * scaled, axis=-1, keepdims=True)
-        stage_b[...] = (
-            cot[...].astype(F32) + inverse * scaled - wide * (inverse * inverse * inverse) * mean
-        ).astype(BF16)
-        m_out_b.start()
+        for h in range(2):
+            rows = pl.ds(64 * h, 64)
+            grads = part[rows, :] + dot(key_value[64 * h:64 * h + 64], wkv[...], NT)
+            scaled = grads * gain[...]
+            wide = xb[rows, :].astype(F32)
+            inverse = lax.rsqrt(jnp.mean(wide * wide, axis=-1, keepdims=True) + NORM_EPSILON)
+            mean = jnp.mean(wide * scaled, axis=-1, keepdims=True)
+            stage_b[rows, :] = (
+                cot[rows, :].astype(F32) + inverse * scaled
+                - wide * (inverse * inverse * inverse) * mean
+            ).astype(BF16)
+            m_out_b[h].start()
 
     def fourth():
         gather_f.wait_x(2)
@@ -430,17 +434,20 @@
     )
     tokens_first(acc[64:128, :] * (1.0 / acc[0:1, :]), ost, att)
     m_att.start()
+    sum_own()
     m_att.wait_recv()
-    stage_f[...] = (
-        xf[...].astype(F32) + dot(jnp.concatenate([att[0], att[1]], axis=1), wo[...], NN)
-    ).astype(BF16)
-    m_out_f.start()
-    sum_own()
+    attended = jnp.concatenate([att[0], att[1]], axis=1)
+    for h in range(2):
+        cols = pl.ds(512 * h, 512)
+        stage_f[:, cols] = (
+            xf[:, cols].astype(F32) + dot(attended, wo[:, cols], NN)
+        ).astype(BF16)
+        m_out_f[h].start()
     finish_backward()
     for copy in used:
         copy.wait_send()
-    m_out_b.wait_recv()
-    m_out_f.wait_recv()
+    for copy in m_out_f + m_out_b:
+        copy.wait_recv()
 
 
 def hand_over(in_f, in_b, out_f, out_b, held, in_sem, out_sem):

time: 74.4 us -> 75 us (level)
  no operation moved by 1% of the time
where the time goes in v4:
time: 75 us; the launch traced here: 74.8 us
  Pallas kernels  74 us (99%)
  between operations  0.8 us (1%)
    pallas_call x1, Pallas kernels, on_device(): pl.pallas_call(fused, out_shape=(shape, shape), in_specs=[any_space] * 3...  72.2 us
    pallas_call x1, Pallas kernels, on_device(): pl.pallas_call(hand_over, out_shape=(shape, shape), in_specs=[any_space]...  1.82 us

profile of v4, /device:TPU:1, one launch (start us, length us, event | category | flops | bytes accessed | tf_op | source)
XLA Modules:
  0.0 74.8 jit_solution(16365252441766996906)
XLA Ops:
  0.6 72.2 %sublayer.1 = (bf16[128,1024]{1,0:T(8,128)(2,1)}, bf16[128,1024]{1,0:T(8,128)(2,1)}) custom-call(bf16[128,1024]{1,0:T(8,128)(2,1)} %bitcast.12, bf16[128,1024]{1,0:T(8,128)(2,1)} %bitcast.13, bf16[128,1024]{1,0:T(8,128)(2,1)} %bitcast.14, f32[1,1024]{1,0:T(1,128)} %gain.1, bf16[1024,512]{1,0:T(8,128)(2,1)} %bitcast.10, bf16[1024,128]{1,0:T(8,128)(2,1)} %bitcast.15, ...), custom_call_target="tpu_custom_call" | custom-call | tf_op jit(solution)/shard_map/sublayer/pallas_call | solution.py:492
  72.8 1.8 %hand_over.1 = (bf16[128,1024]{1,0:T(8,128)(2,1)}, bf16[128,1024]{1,0:T(8,128)(2,1)}) custom-call(bf16[128,1024]{1,0:T(8,128)(2,1)} %get-tuple-element.6.in_f, bf16[128,1024]{1,0:T(8,128)(2,1)} %get-tuple-element.7.in_b), custom_call_target="tpu_custom_call" | custom-call | tf_op jit(solution)/shard_map/hand_over/pallas_call | solution.py:512

commit v5 on v4

--- a/solution.py
+++ b/solution.py
@@ -21,7 +21,7 @@
 
 FORWARD_ORDER = ((0, 0), (0, 1), (1, 0), (3, 0), (2, 0), (2, 1), (1, 1), (3, 1))
 BACKWARD_ORDER = ((2, 1), (2, 0), (1, 1), (1, 0), (3, 1), (3, 0), (0, 1), (0, 0))
-MESSAGES = 63
+MESSAGES = 57
 
 
 def dot(a, b, dims):
@@ -144,7 +144,59 @@
             for copy in self.far[d]:
                 copy.wait_recv()
 
-    gather_b, gather_f = Gather(kvb), Gather(kvf)
+    class WideGather:
+        def __init__(self, kv):
+            own = kv.at[0, 0]
+            self.y = (
+                message(own, kv.at[3, 0], yp), message(own, kv.at[1, 0], ym),
+                message(own, kv.at[2, 0], y2),
+            )
+            self.x = (message(own, kv.at[0, 2], xp), message(own, kv.at[0, 1], xm))
+            self.far = (
+                message(kv.at[0, 2, 0:128], kv.at[0, 3, 0:128], xp),
+                message(kv.at[0, 1, 128:256], kv.at[0, 3, 128:256], xm),
+            )
+            self.row = (
+                message(kv.at[0, 1:4], kv.at[3, 1:4], yp), message(kv.at[0, 1:4], kv.at[1, 1:4], ym),
+            )
+            self.across = (
+                message(kv.at[2, 0], kv.at[2, 2], xp), message(kv.at[2, 0], kv.at[2, 1], xm),
+                message(kv.at[2, 0], kv.at[2, 3], x2),
+            )
+
+        def start_y(self):
+            for copy in self.y:
+                copy.start()
+
+        def start_x(self):
+            for copy in self.x:
+                copy.start()
+
+        def forward(self):
+            for near, far in zip(self.x, self.far):
+                near.wait_recv()
+                far.start()
+
+        def start_row(self):
+            for copy in self.far:
+                copy.wait_recv()
+            for copy in self.row:
+                copy.start()
+
+        def middle(self):
+            self.y[2].wait_recv()
+            for copy in self.across:
+                copy.start()
+
+        def wait_row(self, i):
+            self.y[i].wait_recv()
+            self.row[i].wait_recv()
+
+        def wait_across(self):
+            for copy in self.across:
+                copy.wait_recv()
+
+    gather_b, gather_f = Gather(kvb), WideGather(kvf)
 
     sum_x = {
         (d, p): message(dkv.at[d, p], rx.at[d, p - 1], dev)
@@ -233,7 +285,7 @@
     query_operand(qxb, ws_b)
     gather_b.forward(0)
     m_kvf.wait_recv()
-    gather_f.start_x(0)
+    gather_f.start_x()
     halves(dot(nb[...], wq[...], NN) * 0.125, qst_f, qxf)
     m_qf.start()
     gather_b.near()
@@ -304,22 +356,13 @@
         staged[1] = rows[128:256]
         whole[core] = staged[core]
 
-    def second_row():
-        gather_b.middle()
-        gather_b.forward(1)
-        gather_f.forward(0)
-
-    def third_row():
-        gather_b.forward(3)
-        gather_f.near()
-
     final_max = attention(
         kvb, ws_b,
         {
-            1: lambda: gather_b.wait_far(0),
-            2: second_row,
-            3: third_row,
-            4: lambda: gather_b.wait_x(2),
+            1: lambda: (gather_b.wait_far(0), gather_f.forward()),
+            2: lambda: (gather_b.middle(), gather_b.forward(1)),
+            3: lambda: gather_b.forward(3),
+            4: lambda: (gather_b.wait_x(2), gather_f.start_row()),
             5: lambda: gather_b.wait_far(2),
             6: lambda: (gather_b.wait_far(1), gather_f.middle()),
             7: lambda: gather_b.wait_far(3),
@@ -342,10 +385,6 @@
     accq[...] = jnp.zeros_like(accq)
 
     for t in range(9):
-        if t == 1:
-            gather_f.forward(1)
-        if t == 2:
-            gather_f.forward(3)
         if t == 8:
             add_x(2)
         if t < 8:
@@ -416,19 +455,13 @@
             ).astype(BF16)
             m_out_b[h].start()
 
-    def fourth():
-        gather_f.wait_x(2)
-        add_x(3)
-
     attention(
         kvf, ws_f,
         {
-            1: lambda: (gather_f.wait_far(0), add_x(1)),
-            3: query_part,
-            4: fourth,
-            5: lambda: gather_f.wait_far(2),
-            6: lambda: gather_f.wait_far(1),
-            7: lambda: gather_f.wait_far(3),
+            1: lambda: add_x(1),
+            2: lambda: gather_f.wait_row(1),
+            3: lambda: (gather_f.wait_row(0), query_part()),
+            4: lambda: (gather_f.wait_across(), add_x(3)),
             9: add_own_x,
         },
     )

time: 75 us -> 76.4 us (1.019)
  Pallas kernels: 74 us -> 75.4 us
    pallas_call x1, Pallas kernels: 72.2 us -> 73.6 us  [on_device(): pl.pallas_call(fused, out_shape=(shape, shape), in_specs=[any_space] * 3...]
where the time goes in v5:
time: 76.4 us; the launch traced here: 76.2 us
  Pallas kernels  75.4 us (99%)
  between operations  0.8 us (1%)
    pallas_call x1, Pallas kernels, on_device(): pl.pallas_call(fused, out_shape=(shape, shape), in_specs=[any_space] * 3...  73.6 us
    pallas_call x1, Pallas kernels, on_device(): pl.pallas_call(hand_over, out_shape=(shape, shape), in_specs=[any_space]...  1.82 us

profile of v5, /device:TPU:1, one launch (start us, length us, event | category | flops | bytes accessed | tf_op | source)
XLA Modules:
  0.0 76.2 jit_solution(12770558654264564909)
XLA Ops:
  0.6 73.6 %sublayer.1 = (bf16[128,1024]{1,0:T(8,128)(2,1)}, bf16[128,1024]{1,0:T(8,128)(2,1)}) custom-call(bf16[128,1024]{1,0:T(8,128)(2,1)} %bitcast.12, bf16[128,1024]{1,0:T(8,128)(2,1)} %bitcast.13, bf16[128,1024]{1,0:T(8,128)(2,1)} %bitcast.14, f32[1,1024]{1,0:T(1,128)} %gain.1, bf16[1024,512]{1,0:T(8,128)(2,1)} %bitcast.10, bf16[1024,128]{1,0:T(8,128)(2,1)} %bitcast.15, ...), custom_call_target="tpu_custom_call" | custom-call | tf_op jit(solution)/shard_map/sublayer/pallas_call | solution.py:525
  74.3 1.8 %hand_over.1 = (bf16[128,1024]{1,0:T(8,128)(2,1)}, bf16[128,1024]{1,0:T(8,128)(2,1)}) custom-call(bf16[128,1024]{1,0:T(8,128)(2,1)} %get-tuple-element.6.in_f, bf16[128,1024]{1,0:T(8,128)(2,1)} %get-tuple-element.7.in_b), custom_call_target="tpu_custom_call" | custom-call | tf_op jit(solution)/shard_map/hand_over/pallas_call | solution.py:545

commit v6 on v4

--- a/solution.py
+++ b/solution.py
@@ -309,8 +309,8 @@
         gather_b.forward(1)
         gather_f.forward(0)
 
-    def third_row():
-        gather_b.forward(3)
+    def last_b():
+        gather_b.wait_far(1)
         gather_f.near()
 
     final_max = attention(
@@ -318,11 +318,12 @@
         {
             1: lambda: gather_b.wait_far(0),
             2: second_row,
-            3: third_row,
+            3: lambda: gather_b.forward(3),
             4: lambda: gather_b.wait_x(2),
             5: lambda: gather_b.wait_far(2),
-            6: lambda: (gather_b.wait_far(1), gather_f.middle()),
+            6: last_b,
             7: lambda: gather_b.wait_far(3),
+            8: gather_f.middle,
         },
     )
     inverse_sum = 1.0 / acc[0:1, :]
@@ -342,9 +343,9 @@
     accq[...] = jnp.zeros_like(accq)
 
     for t in range(9):
-        if t == 1:
+        if t == 4:
             gather_f.forward(1)
-        if t == 2:
+        if t == 5:
             gather_f.forward(3)
         if t == 8:
             add_x(2)
@@ -416,25 +417,20 @@
             ).astype(BF16)
             m_out_b[h].start()
 
-    def fourth():
-        gather_f.wait_x(2)
-        add_x(3)
-
     attention(
         kvf, ws_f,
         {
             1: lambda: (gather_f.wait_far(0), add_x(1)),
-            3: query_part,
-            4: fourth,
+            3: lambda: add_x(3),
+            4: lambda: gather_f.wait_x(2),
             5: lambda: gather_f.wait_far(2),
             6: lambda: gather_f.wait_far(1),
-            7: lambda: gather_f.wait_far(3),
+            7: lambda: (gather_f.wait_far(3), query_part()),
             9: add_own_x,
         },
     )
     tokens_first(acc[64:128, :] * (1.0 / acc[0:1, :]), ost, att)
     m_att.start()
-    sum_own()
     m_att.wait_recv()
     attended = jnp.concatenate([att[0], att[1]], axis=1)
     for h in range(2):
@@ -443,6 +439,8 @@
             xf[:, cols].astype(F32) + dot(attended, wo[:, cols], NN)
         ).astype(BF16)
         m_out_f[h].start()
+        if h == 0:
+            sum_own()
     finish_backward()
     for copy in used:
         copy.wait_send()

time: 75 us -> 74.2 us (0.989)
  Pallas kernels: 74 us -> 73.2 us
    pallas_call x1, Pallas kernels: 72.2 us -> 71.4 us  [on_device(): pl.pallas_call(fused, out_shape=(shape, shape), in_specs=[any_space] * 3...]
where the time goes in v6:
time: 74.2 us; the launch traced here: 74 us
  Pallas kernels  73.2 us (99%)
  between operations  0.8 us (1%)
    pallas_call x1, Pallas kernels, on_device(): pl.pallas_call(fused, out_shape=(shape, shape), in_specs=[any_space] * 3...  71.4 us
    pallas_call x1, Pallas kernels, on_device(): pl.pallas_call(hand_over, out_shape=(shape, shape), in_specs=[any_space]...  1.82 us

profile of v6, /device:TPU:1, one launch (start us, length us, event | category | flops | bytes accessed | tf_op | source)
XLA Modules:
  0.0 74.0 jit_solution(11177168831563230788)
XLA Ops:
  0.6 71.4 %sublayer.1 = (bf16[128,1024]{1,0:T(8,128)(2,1)}, bf16[128,1024]{1,0:T(8,128)(2,1)}) custom-call(bf16[128,1024]{1,0:T(8,128)(2,1)} %bitcast.12, bf16[128,1024]{1,0:T(8,128)(2,1)} %bitcast.13, bf16[128,1024]{1,0:T(8,128)(2,1)} %bitcast.14, f32[1,1024]{1,0:T(1,128)} %gain.1, bf16[1024,512]{1,0:T(8,128)(2,1)} %bitcast.10, bf16[1024,128]{1,0:T(8,128)(2,1)} %bitcast.15, ...), custom_call_target="tpu_custom_call" | custom-call | tf_op jit(solution)/shard_map/sublayer/pallas_call | solution.py:490
  72.0 1.8 %hand_over.1 = (bf16[128,1024]{1,0:T(8,128)(2,1)}, bf16[128,1024]{1,0:T(8,128)(2,1)}) custom-call(bf16[128,1024]{1,0:T(8,128)(2,1)} %get-tuple-element.6.in_f, bf16[128,1024]{1,0:T(8,128)(2,1)} %get-tuple-element.7.in_b), custom_call_target="tpu_custom_call" | custom-call | tf_op jit(solution)/shard_map/hand_over/pallas_call | solution.py:510
